TPU v7x, 128 devices: a whole 4x4x4 slice. The times are simulated.
128 devices in a mesh: inner: 16 (over x_hi, y, core), outer: 8 (over x_lo, z).
Axes of the slice: x: 4 (x_hi: 2, x_lo: 2; x = x_hi * 2 + x_lo), y: 4, z: 4, core: 2. Of those that a mesh axis runs over, the one named last changes fastest.
Arguments:
- hidden_in: bfloat16 [16384, 4096], P(('inner', 'outer')), may hold values from -6 to 6
- queries: bfloat16 [16384, 2048], P(('inner', 'outer')), may hold values from -6 to 6
- keys: bfloat16 [16384, 512], P(('inner', 'outer')), may hold values from -6 to 6
- values: bfloat16 [16384, 512], P(('inner', 'outer')), may hold values from -6 to 6
- attention_output: bfloat16 [16384, 2048], P(('inner', 'outer')), may hold values from -6 to 6
- output_gradient: bfloat16 [16384, 2048], P(('inner', 'outer')), may hold values from -6 to 6
- log_softmax_total: float32 [16384, 16], P(('inner', 'outer')), may hold values from 0 to 20
- positions: int32 [16384], P(('inner', 'outer')), may hold values from 0 to 16383, as said below
Outputs:
- grad_queries: bfloat16 [16384, 2048], P(('inner', 'outer'))
- grad_wk: float32 [4096, 512], replicated
- grad_wv: float32 [4096, 512], replicated
Inputs may be any that keep to these rules, and one draw needn't show every extreme that they name: Each device's 128 rows form two runs of 64 consecutive positions, each starting at a multiple of 64; every position occurs once.
All inputs are finite; a program needn't handle non-finite values.
Results may differ from a plain program's by a relative error of at most 0.0052.
Values may be sent and summed in bfloat16 or wider, within the bound.
A program may use at most 320 MiB of HBM per device.

v0:
```python
import jax
import jax.numpy as jnp
from jax import lax
from jax.sharding import PartitionSpec as P

QUERY_HEADS = 16
KEY_VALUE_HEADS = 4
HEAD_SIZE = 128


def shortened(value):

    def short(part):
        return part.astype(jnp.bfloat16) if part.dtype == jnp.float32 else part

    return jax.tree.map(short, value)


def from_behind(value, axis, by):
    length = lax.axis_size(axis)
    return lax.ppermute(value, axis, [(i, (i + by) % length) for i in range(length)])


def rows_via_outer(blocks):
    return jax.tree.map(
        lambda part, own: part.astype(own.dtype), from_behind(shortened(blocks), "outer", 1), blocks
    )


def stats_via_outer(blocks):
    return from_behind(blocks, "outer", 1)


def local(
    hidden_in,
    queries,
    keys,
    values,
    attention_output,
    output_gradient,
    log_softmax_total,
    positions,
):
    query_group = QUERY_HEADS // KEY_VALUE_HEADS
    scale = HEAD_SIZE ** (-0.5)
    token_rows = queries.shape[0]
    gradient_whole = output_gradient.reshape(
        token_rows, KEY_VALUE_HEADS, query_group, HEAD_SIZE
    ).astype(jnp.float32)
    output_whole = attention_output.reshape(
        token_rows, KEY_VALUE_HEADS, query_group, HEAD_SIZE
    ).astype(jnp.float32)
    delta_own = jnp.sum(gradient_whole * output_whole, axis=-1).reshape(token_rows, QUERY_HEADS)

    def attend(
        query_slice,
        gradient_slice,
        logsumexp_slice,
        delta_slice,
        qplace,
        key_slice,
        value_slice,
        kplace,
    ):
        block_count = query_slice.shape[0]
        row_extent = key_slice.shape[0]
        query_per_head = query_slice.reshape(block_count, KEY_VALUE_HEADS, query_group, HEAD_SIZE)
        gradient_per_head = gradient_slice.reshape(
            block_count, KEY_VALUE_HEADS, query_group, HEAD_SIZE
        )
        logsumexp_per_head = logsumexp_slice.reshape(
            block_count, KEY_VALUE_HEADS, query_group
        ).transpose(1, 2, 0)[..., None]
        delta_per_head = delta_slice.reshape(block_count, KEY_VALUE_HEADS, query_group).transpose(
            1, 2, 0
        )[..., None]
        key_per_head = key_slice.reshape(row_extent, KEY_VALUE_HEADS, HEAD_SIZE)
        value_per_head = value_slice.reshape(row_extent, KEY_VALUE_HEADS, HEAD_SIZE)
        scores = (
            jnp.einsum(
                "qgrd,kgd->grqk", query_per_head, key_per_head, preferred_element_type=jnp.float32
            )
            * scale
        )
        allowed = kplace[None, :] <= qplace[:, None]
        probs = jnp.where(allowed, jnp.exp(scores - logsumexp_per_head), 0.0)
        dprobs = jnp.einsum(
            "qgrd,kgd->grqk", gradient_per_head, value_per_head, preferred_element_type=jnp.float32
        )
        dscores = (probs * (dprobs - delta_per_head)).astype(jnp.bfloat16)
        probs_low = probs.astype(jnp.bfloat16)
        part_q = (
            jnp.einsum("grqk,kgd->qgrd", dscores, key_per_head, preferred_element_type=jnp.float32)
            * scale
        )
        slice_keys = (
            jnp.einsum(
                "grqk,qgrd->kgd", dscores, query_per_head, preferred_element_type=jnp.float32
            )
            * scale
        )
        slice_values = jnp.einsum(
            "grqk,qgrd->kgd", probs_low, gradient_per_head, preferred_element_type=jnp.float32
        )
        return (
            part_q.reshape(block_count, QUERY_HEADS * HEAD_SIZE),
            slice_keys.reshape(row_extent, KEY_VALUE_HEADS * HEAD_SIZE),
            slice_values.reshape(row_extent, KEY_VALUE_HEADS * HEAD_SIZE),
        )

    def examine(
        query_slice,
        gradient_slice,
        logsumexp_slice,
        delta_slice,
        qplace,
        key_slice,
        value_slice,
        kplace,
    ):
        return attend(
            query_slice,
            gradient_slice,
            logsumexp_slice,
            delta_slice,
            qplace,
            key_slice,
            value_slice,
            kplace,
        )

    all_keys, all_values = (
        lax.all_gather(keys, "inner", axis=0, tiled=True),
        lax.all_gather(values, "inner", axis=0, tiled=True),
    )
    all_places = lax.all_gather(positions, "inner", axis=0, tiled=True)
    total = all_keys.shape[0]
    key_extent = min(512, total)
    span_count = total // key_extent
    places_f = all_places.astype(jnp.float32)

    def advance(counter, current):
        query_slice, gradient_slice, stats, sums = current
        logsumexp_slice, delta_slice, qplace, acc_q = stats
        new_sums = []
        for piece_index in range(span_count):
            lower = piece_index * key_extent
            part_q, slice_keys, slice_values = examine(
                query_slice,
                gradient_slice,
                logsumexp_slice,
                delta_slice,
                qplace,
                all_keys[lower : lower + key_extent],
                all_values[lower : lower + key_extent],
                places_f[lower : lower + key_extent],
            )
            acc_q = acc_q + part_q
            new_sums.append(
                (sums[piece_index][0] + slice_keys, sums[piece_index][1] + slice_values)
            )
        query_slice, gradient_slice = rows_via_outer((query_slice, gradient_slice))
        stats = stats_via_outer((logsumexp_slice, delta_slice, qplace, acc_q))
        return (query_slice, gradient_slice, stats, tuple(new_sums))

    blank_buffer = jnp.zeros((key_extent, KEY_VALUE_HEADS * HEAD_SIZE), jnp.float32)
    start_sums = tuple(((blank_buffer, blank_buffer) for piece_index in range(span_count)))
    start_stats = (
        log_softmax_total,
        delta_own,
        positions.astype(jnp.float32),
        jnp.zeros((token_rows, QUERY_HEADS * HEAD_SIZE), jnp.float32),
    )
    final = lax.fori_loop(
        0, lax.axis_size("outer"), advance, (queries, output_gradient, start_stats, start_sums)
    )
    sums = final[3]
    sum_keys = jnp.concatenate([pair[0] for pair in sums], axis=0)
    sum_values = jnp.concatenate([pair[1] for pair in sums], axis=0)
    acc_q, sum_keys, sum_values = (final[2][3], sum_keys, sum_values)
    own_k, own_v = (
        lax.psum_scatter(sum_keys, "inner", scatter_dimension=0, tiled=True),
        lax.psum_scatter(sum_values, "inner", scatter_dimension=0, tiled=True),
    )
    grad_queries = acc_q.astype(jnp.bfloat16)
    term_k = jnp.dot(hidden_in.T, own_k.astype(jnp.bfloat16), preferred_element_type=jnp.float32)
    term_v = jnp.dot(hidden_in.T, own_v.astype(jnp.bfloat16), preferred_element_type=jnp.float32)
    grad_wk, grad_wv = lax.psum((term_k, term_v), ("inner", "outer"))
    return (grad_queries, grad_wk, grad_wv)


def solution(mesh):
    placed = (
        P(("inner", "outer"), None),
        P(("inner", "outer"), None),
        P(("inner", "outer"), None),
        P(("inner", "outer"), None),
        P(("inner", "outer"), None),
        P(("inner", "outer"), None),
        P(("inner", "outer"), None),
        P(("inner", "outer")),
    )
    return jax.shard_map(
        local,
        mesh=mesh,
        in_specs=placed,
        out_specs=(P(("inner", "outer"), None), P(), P()),
        check_vma=False,
    )
```

profile of v0, /device:TPU:1, one launch (start us, length us, event | category | flops | bytes accessed | tf_op | source)
XLA Modules:
  0.0 1005.6 jit_solution(4886945492538978614)
XLA Ops:
  11.5 25.7 %all-gather = s32[16,1,128]{2,1,0:T(1,128)S(1)} all-gather(s32[1,1,128]{2,1,0:T(1,128)} %bitcast.437), channel_id=1, replica_groups=mesh['inner'=16,'outer'=8] {'inner'}, dimensions={0}, use_global_device_ids=true | all-gather | bytes 8704 | tf_op jit(solution)/shard_map/all_gather | solution.py:136
  45.8 15.6 %all-gather.4.cloned.1.call-done = bf16[2048,512]{0,1:T(8,128)(2,1)} async-done(((bf16[128,512]{0,1:T(8,128)(2,1)}), bf16[2048,512]{0,1:T(8,128)(2,1)}) %all-gather.4.cloned.1.call-update) | async-done | bytes 2097168 | tf_op jit(solution)/shard_map/all_gather | solution.py:133
  61.4 48.0 %all-gather.6.cloned.1.call-done = bf16[2048,512]{0,1:T(8,128)(2,1)} async-done(((bf16[128,512]{0,1:T(8,128)(2,1)}), bf16[2048,512]{0,1:T(8,128)(2,1)}) %all-gather.6.cloned.1.call-update) | async-done | bytes 2097168 | tf_op jit(solution)/shard_map/all_gather | solution.py:134
  110.4 465.6 %while.37 = (s32[]{:T(128)}, bf16[128,2048]{0,1:T(8,128)(2,1)S(1)}, bf16[128,2048]{0,1:T(8,128)(2,1)}, f32[128,16]{0,1:T(8,128)S(1)}, f32[128,16]{0,1:T(8,128)S(...) while((s32[]{:T(128)}, bf16[128,2048]{0,1:T(8,128)(2,1)S(1)}, ...), condition=%wide.region_2.3_spmd.clone, body=%wide.region_1.2_spmd.clone.sunk | while | flops 5418254336 | bytes 212824336 | solution.py:174
  137.3 3.0 fusion.217
  142.0 3.0 fusion.219
  146.9 3.0 fusion.215
  150.7 3.0 fusion.213
  153.7 3.6 bitcast_add_fusion.20
  198.2 3.0 fusion.219
  203.0 3.0 fusion.215
  206.8 3.0 fusion.213
  209.8 4.2 bitcast_add_fusion.20
  214.0 3.5 bitcast_add_fusion.21
  220.5 3.4 bitcast_add_fusion.18
  251.2 3.0 fusion.217
  256.0 3.0 fusion.219
  260.8 3.0 fusion.215
  264.6 3.0 fusion.213
  267.6 4.2 bitcast_add_fusion.20
  271.8 3.5 bitcast_add_fusion.21
  280.9 3.4 bitcast_add_fusion.18
  314.8 3.0 fusion.219
  319.6 3.0 fusion.215
  323.4 3.0 fusion.213
  326.4 4.2 bitcast_add_fusion.20
  330.7 3.5 bitcast_add_fusion.21
  338.2 3.4 bitcast_add_fusion.18
  373.0 3.0 fusion.219
  377.9 3.0 fusion.215
  381.7 3.0 fusion.213
  384.7 4.2 bitcast_add_fusion.20
  388.9 3.5 bitcast_add_fusion.21
  397.5 3.4 bitcast_add_fusion.18
  427.5 3.0 fusion.217
  432.3 3.0 fusion.219
  437.1 3.0 fusion.215
  440.9 3.0 fusion.213
  444.0 4.2 bitcast_add_fusion.20
  448.2 3.5 bitcast_add_fusion.21
  455.8 3.4 bitcast_add_fusion.18
  485.3 3.0 fusion.217
  490.1 3.0 fusion.219
  494.9 3.0 fusion.215
  498.7 3.0 fusion.213
  501.7 4.2 bitcast_add_fusion.20
  506.0 3.5 bitcast_add_fusion.21
  515.0 3.4 bitcast_add_fusion.18
  544.2 3.0 fusion.217
  548.9 3.0 fusion.219
  553.7 3.0 fusion.215
  557.6 3.0 fusion.213
  560.6 4.2 bitcast_add_fusion.20
  564.8 3.5 bitcast_add_fusion.21
  572.4 3.4 bitcast_add_fusion.18
  576.1 4.6 pad_maximum_fusion.1
  582.2 4.0 pad_maximum_fusion
  586.3 86.9 %reduce-scatter.5.cloned.1.call-done = f32[128,512]{0,1:T(8,128)} async-done(((f32[2048,512]{0,1:T(8,128)}), f32[128,512]{0,1:T(8,128)}) %reduce-scatter.5.cloned.1.call-update) | async-done | bytes 262160 | tf_op jit(solution)/shard_map/reduce_scatter | solution.py:183
  673.2 5.6 convolution_bitcast_fusion.4
  678.8 78.7 %reduce-scatter.3.cloned.1.call-done = f32[128,512]{0,1:T(8,128)} async-done(((f32[2048,512]{0,1:T(8,128)}), f32[128,512]{0,1:T(8,128)}) %reduce-scatter.3.cloned.1.call-update) | async-done | bytes 262160 | tf_op jit(solution)/shard_map/reduce_scatter | solution.py:182
  757.5 5.6 convolution_bitcast_fusion.5
  765.4 215.8 %all-reduce.3.cloned.1.call-done = (f32[4096,512]{0,1:T(8,128)}, f32[4096,512]{0,1:T(8,128)}) async-done(((f32[4096,512]{0,1:T(8,128)}, f32[4096,512]{0,1:T(8,128)}), (f32[4096,512]{0,1:T(8,128)}, f32[4096,512]{0,1:T(8,128)})) %all-reduce.3.cloned.1.call-update) | async-done | bytes 16777232 | tf_op jit(solution)/shard_map/psum | solution.py:188
  981.2 8.9 copy.145
  990.1 8.9 copy.146
  (531 shorter events, 312.8 us)
Async XLA Ops:
  7.2 666.0 %copy-start = (bf16[128,4096]{1,0:T(8,128)(2,1)S(1)}, bf16[128,4096]{1,0:T(8,128)(2,1)}, u32[]{:S(2)}) copy-start(bf16[128,4096]{1,0:T(8,128)(2,1)} %param.10) | copy-start | bytes 3145732
  7.2 54.2 %all-gather.4.cloned.1.call-start = ((), (), s32[]{:S(2)}) async-start(), calls=%async_computation.2 | async-start | bytes 2228224 | tf_op jit(solution)/shard_map/all_gather | solution.py:133
  9.0 100.4 %all-gather.6.cloned.1.call-start = ((), (), s32[]{:S(2)}) async-start(), calls=%async_computation.3 | async-start | bytes 2228224 | tf_op jit(solution)/shard_map/all_gather | solution.py:134
  10.7 662.5 %reduce-scatter.5.cloned.1.call-start = ((), (), s32[]{:S(2)}) async-start(), calls=%async_computation.5 | async-start | bytes 4456448 | tf_op jit(solution)/shard_map/reduce_scatter | solution.py:183
  38.6 71.8 %copy-start.14 = (f32[128,16]{0,1:T(8,128)S(1)}, f32[128,16]{0,1:T(8,128)}, u32[]{:S(2)}) copy-start(f32[128,16]{0,1:T(8,128)} %param.16) | copy-start | bytes 24580
  110.4 7.3 copy-start.4
  110.4 51.5 %collective-permute-start.4 = (f32[128]{0:T(128)S(1)}, f32[128]{0:T(128)S(1)}, u32[]{:S(2)}, u32[]{:S(2)}) collective-permute-start(f32[128]{0:T(128)S(1)} %copy.223), channel_id=1, source_target_pairs={{0,1},{1,2},{2,3},{3,4},{4,5},{5,6},{6,7},{7,0},{8,9},{9,10},{10,1... | collective-permute-start | bytes 1544 | tf_op jit(solution)/shard_map/while/body/eval_jaxpr/ppermute | solution.py:21
  111.8 53.6 %collective-permute-start.2 = (f32[128,16]{0,1:T(8,128)S(1)}, f32[128,16]{0,1:T(8,128)S(1)}, u32[]{:S(2)}, u32[]{:S(2)}) collective-permute-start(f32[128,16]{0,1:T(8,128)S(1)} %copy.221), channel_id=1, source_target_pairs={{0,1},{1,2},{2,3},{3,4},{4,5},{5,6},{6,7},{7,0},{8,9},{9,10},{10,1... | collective-permute-start | bytes 24584 | tf_op jit(solution)/shard_map/while/body/eval_jaxpr/ppermute | solution.py:21
  113.1 53.7 %collective-permute-start = (bf16[128,2048]{0,1:T(8,128)(2,1)S(1)}, bf16[128,2048]{0,1:T(8,128)(2,1)S(1)}, u32[]{:S(2)}, u32[]{:S(2)}) collective-permute-start(bf16[128,2048]{0,1:T(8,128)(2,1)S(1)} %copy.219), channel_id=1, source_target_pairs={{0,1},{1,2},{2,3},{3,4},{4,5},{5,6},{6,7},{7,0},{8,9},{9,10},{10,1... | collective-permute-start | bytes 1572872 | tf_op jit(solution)/shard_map/while/body/eval_jaxpr/ppermute | solution.py:21
  116.0 50.8 %collective-permute-start.1 = (bf16[128,2048]{0,1:T(8,128)(2,1)}, bf16[128,2048]{0,1:T(8,128)(2,1)}, u32[]{:S(2)}, u32[]{:S(2)}) collective-permute-start(bf16[128,2048]{0,1:T(8,128)(2,1)} %copy.220), channel_id=1, source_target_pairs={{0,1},{1,2},{2,3},{3,4},{4,5},{5,6},{6,7},{7,0},{8,9},{9,10},{10,1... | collective-permute-start | bytes 1572872 | tf_op jit(solution)/shard_map/while/body/eval_jaxpr/ppermute | solution.py:21
  136.1 30.7 %collective-permute-start.5 = (f32[128,2048]{0,1:T(8,128)}, f32[128,2048]{0,1:T(8,128)}, u32[]{:S(2)}, u32[]{:S(2)}) collective-permute-start(f32[128,2048]{0,1:T(8,128)} %bitcast_add_fusion.17), channel_id=1, source_target_pairs={{0,1},{1,2},{2,3},{3,4},{4,5},{5,6},{6,7},{7,0},{8,9},{9,10},{10,1... | collective-permute-start | bytes 3145736 | tf_op jit(solution)/shard_map/while/body/eval_jaxpr/ppermute | solution.py:21
  162.2 4.6 collective-permute-start.3
  166.8 8.2 copy-start.4
  166.8 53.4 %collective-permute-start.4 = (f32[128]{0:T(128)S(1)}, f32[128]{0:T(128)S(1)}, u32[]{:S(2)}, u32[]{:S(2)}) collective-permute-start(f32[128]{0:T(128)S(1)} %copy.223), channel_id=1, source_target_pairs={{0,1},{1,2},{2,3},{3,4},{4,5},{5,6},{6,7},{7,0},{8,9},{9,10},{10,1... | collective-permute-start | bytes 1544 | tf_op jit(solution)/shard_map/while/body/eval_jaxpr/ppermute | solution.py:21
  166.9 57.0 %collective-permute-start.2 = (f32[128,16]{0,1:T(8,128)S(1)}, f32[128,16]{0,1:T(8,128)S(1)}, u32[]{:S(2)}, u32[]{:S(2)}) collective-permute-start(f32[128,16]{0,1:T(8,128)S(1)} %copy.221), channel_id=1, source_target_pairs={{0,1},{1,2},{2,3},{3,4},{4,5},{5,6},{6,7},{7,0},{8,9},{9,10},{10,1... | collective-permute-start | bytes 24584 | tf_op jit(solution)/shard_map/while/body/eval_jaxpr/ppermute | solution.py:21
  167.5 57.6 %collective-permute-start = (bf16[128,2048]{0,1:T(8,128)(2,1)S(1)}, bf16[128,2048]{0,1:T(8,128)(2,1)S(1)}, u32[]{:S(2)}, u32[]{:S(2)}) collective-permute-start(bf16[128,2048]{0,1:T(8,128)(2,1)S(1)} %copy.219), channel_id=1, source_target_pairs={{0,1},{1,2},{2,3},{3,4},{4,5},{5,6},{6,7},{7,0},{8,9},{9,10},{10,1... | collective-permute-start | bytes 1572872 | tf_op jit(solution)/shard_map/while/body/eval_jaxpr/ppermute | solution.py:21
  170.7 54.4 %collective-permute-start.1 = (bf16[128,2048]{0,1:T(8,128)(2,1)}, bf16[128,2048]{0,1:T(8,128)(2,1)}, u32[]{:S(2)}, u32[]{:S(2)}) collective-permute-start(bf16[128,2048]{0,1:T(8,128)(2,1)} %copy.220), channel_id=1, source_target_pairs={{0,1},{1,2},{2,3},{3,4},{4,5},{5,6},{6,7},{7,0},{8,9},{9,10},{10,1... | collective-permute-start | bytes 1572872 | tf_op jit(solution)/shard_map/while/body/eval_jaxpr/ppermute | solution.py:21
  193.3 31.8 %collective-permute-start.5 = (f32[128,2048]{0,1:T(8,128)}, f32[128,2048]{0,1:T(8,128)}, u32[]{:S(2)}, u32[]{:S(2)}) collective-permute-start(f32[128,2048]{0,1:T(8,128)} %bitcast_add_fusion.17), channel_id=1, source_target_pairs={{0,1},{1,2},{2,3},{3,4},{4,5},{5,6},{6,7},{7,0},{8,9},{9,10},{10,1... | collective-permute-start | bytes 3145736 | tf_op jit(solution)/shard_map/while/body/eval_jaxpr/ppermute | solution.py:21
  220.4 4.6 collective-permute-start.3
  225.1 7.3 copy-start.4
  225.1 52.9 %collective-permute-start.4 = (f32[128]{0:T(128)S(1)}, f32[128]{0:T(128)S(1)}, u32[]{:S(2)}, u32[]{:S(2)}) collective-permute-start(f32[128]{0:T(128)S(1)} %copy.223), channel_id=1, source_target_pairs={{0,1},{1,2},{2,3},{3,4},{4,5},{5,6},{6,7},{7,0},{8,9},{9,10},{10,1... | collective-permute-start | bytes 1544 | tf_op jit(solution)/shard_map/while/body/eval_jaxpr/ppermute | solution.py:21
  225.2 59.1 %collective-permute-start.2 = (f32[128,16]{0,1:T(8,128)S(1)}, f32[128,16]{0,1:T(8,128)S(1)}, u32[]{:S(2)}, u32[]{:S(2)}) collective-permute-start(f32[128,16]{0,1:T(8,128)S(1)} %copy.221), channel_id=1, source_target_pairs={{0,1},{1,2},{2,3},{3,4},{4,5},{5,6},{6,7},{7,0},{8,9},{9,10},{10,1... | collective-permute-start | bytes 24584 | tf_op jit(solution)/shard_map/while/body/eval_jaxpr/ppermute | solution.py:21
  227.5 56.8 %collective-permute-start = (bf16[128,2048]{0,1:T(8,128)(2,1)S(1)}, bf16[128,2048]{0,1:T(8,128)(2,1)S(1)}, u32[]{:S(2)}, u32[]{:S(2)}) collective-permute-start(bf16[128,2048]{0,1:T(8,128)(2,1)S(1)} %copy.219), channel_id=1, source_target_pairs={{0,1},{1,2},{2,3},{3,4},{4,5},{5,6},{6,7},{7,0},{8,9},{9,10},{10,1... | collective-permute-start | bytes 1572872 | tf_op jit(solution)/shard_map/while/body/eval_jaxpr/ppermute | solution.py:21
  229.5 54.8 %collective-permute-start.1 = (bf16[128,2048]{0,1:T(8,128)(2,1)}, bf16[128,2048]{0,1:T(8,128)(2,1)}, u32[]{:S(2)}, u32[]{:S(2)}) collective-permute-start(bf16[128,2048]{0,1:T(8,128)(2,1)} %copy.220), channel_id=1, source_target_pairs={{0,1},{1,2},{2,3},{3,4},{4,5},{5,6},{6,7},{7,0},{8,9},{9,10},{10,1... | collective-permute-start | bytes 1572872 | tf_op jit(solution)/shard_map/while/body/eval_jaxpr/ppermute | solution.py:21
  250.6 33.7 %collective-permute-start.5 = (f32[128,2048]{0,1:T(8,128)}, f32[128,2048]{0,1:T(8,128)}, u32[]{:S(2)}, u32[]{:S(2)}) collective-permute-start(f32[128,2048]{0,1:T(8,128)} %bitcast_add_fusion.17), channel_id=1, source_target_pairs={{0,1},{1,2},{2,3},{3,4},{4,5},{5,6},{6,7},{7,0},{8,9},{9,10},{10,1... | collective-permute-start | bytes 3145736 | tf_op jit(solution)/shard_map/while/body/eval_jaxpr/ppermute | solution.py:21
  278.2 6.1 collective-permute-start.3
  284.3 7.3 copy-start.4
  284.4 52.5 %collective-permute-start.4 = (f32[128]{0:T(128)S(1)}, f32[128]{0:T(128)S(1)}, u32[]{:S(2)}, u32[]{:S(2)}) collective-permute-start(f32[128]{0:T(128)S(1)} %copy.223), channel_id=1, source_target_pairs={{0,1},{1,2},{2,3},{3,4},{4,5},{5,6},{6,7},{7,0},{8,9},{9,10},{10,1... | collective-permute-start | bytes 1544 | tf_op jit(solution)/shard_map/while/body/eval_jaxpr/ppermute | solution.py:21
  284.5 57.1 %collective-permute-start.2 = (f32[128,16]{0,1:T(8,128)S(1)}, f32[128,16]{0,1:T(8,128)S(1)}, u32[]{:S(2)}, u32[]{:S(2)}) collective-permute-start(f32[128,16]{0,1:T(8,128)S(1)} %copy.221), channel_id=1, source_target_pairs={{0,1},{1,2},{2,3},{3,4},{4,5},{5,6},{6,7},{7,0},{8,9},{9,10},{10,1... | collective-permute-start | bytes 24584 | tf_op jit(solution)/shard_map/while/body/eval_jaxpr/ppermute | solution.py:21
  285.7 55.9 %collective-permute-start = (bf16[128,2048]{0,1:T(8,128)(2,1)S(1)}, bf16[128,2048]{0,1:T(8,128)(2,1)S(1)}, u32[]{:S(2)}, u32[]{:S(2)}) collective-permute-start(bf16[128,2048]{0,1:T(8,128)(2,1)S(1)} %copy.219), channel_id=1, source_target_pairs={{0,1},{1,2},{2,3},{3,4},{4,5},{5,6},{6,7},{7,0},{8,9},{9,10},{10,1... | collective-permute-start | bytes 1572872 | tf_op jit(solution)/shard_map/while/body/eval_jaxpr/ppermute | solution.py:21
  287.8 53.9 %collective-permute-start.1 = (bf16[128,2048]{0,1:T(8,128)(2,1)}, bf16[128,2048]{0,1:T(8,128)(2,1)}, u32[]{:S(2)}, u32[]{:S(2)}) collective-permute-start(bf16[128,2048]{0,1:T(8,128)(2,1)} %copy.220), channel_id=1, source_target_pairs={{0,1},{1,2},{2,3},{3,4},{4,5},{5,6},{6,7},{7,0},{8,9},{9,10},{10,1... | collective-permute-start | bytes 1572872 | tf_op jit(solution)/shard_map/while/body/eval_jaxpr/ppermute | solution.py:21
  309.9 31.8 %collective-permute-start.5 = (f32[128,2048]{0,1:T(8,128)}, f32[128,2048]{0,1:T(8,128)}, u32[]{:S(2)}, u32[]{:S(2)}) collective-permute-start(f32[128,2048]{0,1:T(8,128)} %bitcast_add_fusion.17), channel_id=1, source_target_pairs={{0,1},{1,2},{2,3},{3,4},{4,5},{5,6},{6,7},{7,0},{8,9},{9,10},{10,1... | collective-permute-start | bytes 3145736 | tf_op jit(solution)/shard_map/while/body/eval_jaxpr/ppermute | solution.py:21
  337.1 4.6 collective-permute-start.3
  341.7 8.2 copy-start.4
  341.7 53.4 %collective-permute-start.4 = (f32[128]{0:T(128)S(1)}, f32[128]{0:T(128)S(1)}, u32[]{:S(2)}, u32[]{:S(2)}) collective-permute-start(f32[128]{0:T(128)S(1)} %copy.223), channel_id=1, source_target_pairs={{0,1},{1,2},{2,3},{3,4},{4,5},{5,6},{6,7},{7,0},{8,9},{9,10},{10,1... | collective-permute-start | bytes 1544 | tf_op jit(solution)/shard_map/while/body/eval_jaxpr/ppermute | solution.py:21
  342.3 58.6 %collective-permute-start.2 = (f32[128,16]{0,1:T(8,128)S(1)}, f32[128,16]{0,1:T(8,128)S(1)}, u32[]{:S(2)}, u32[]{:S(2)}) collective-permute-start(f32[128,16]{0,1:T(8,128)S(1)} %copy.221), channel_id=1, source_target_pairs={{0,1},{1,2},{2,3},{3,4},{4,5},{5,6},{6,7},{7,0},{8,9},{9,10},{10,1... | collective-permute-start | bytes 24584 | tf_op jit(solution)/shard_map/while/body/eval_jaxpr/ppermute | solution.py:21
  345.0 55.9 %collective-permute-start = (bf16[128,2048]{0,1:T(8,128)(2,1)S(1)}, bf16[128,2048]{0,1:T(8,128)(2,1)S(1)}, u32[]{:S(2)}, u32[]{:S(2)}) collective-permute-start(bf16[128,2048]{0,1:T(8,128)(2,1)S(1)} %copy.219), channel_id=1, source_target_pairs={{0,1},{1,2},{2,3},{3,4},{4,5},{5,6},{6,7},{7,0},{8,9},{9,10},{10,1... | collective-permute-start | bytes 1572872 | tf_op jit(solution)/shard_map/while/body/eval_jaxpr/ppermute | solution.py:21
  347.0 53.9 %collective-permute-start.1 = (bf16[128,2048]{0,1:T(8,128)(2,1)}, bf16[128,2048]{0,1:T(8,128)(2,1)}, u32[]{:S(2)}, u32[]{:S(2)}) collective-permute-start(bf16[128,2048]{0,1:T(8,128)(2,1)} %copy.220), channel_id=1, source_target_pairs={{0,1},{1,2},{2,3},{3,4},{4,5},{5,6},{6,7},{7,0},{8,9},{9,10},{10,1... | collective-permute-start | bytes 1572872 | tf_op jit(solution)/shard_map/while/body/eval_jaxpr/ppermute | solution.py:21
  368.2 32.8 %collective-permute-start.5 = (f32[128,2048]{0,1:T(8,128)}, f32[128,2048]{0,1:T(8,128)}, u32[]{:S(2)}, u32[]{:S(2)}) collective-permute-start(f32[128,2048]{0,1:T(8,128)} %bitcast_add_fusion.17), channel_id=1, source_target_pairs={{0,1},{1,2},{2,3},{3,4},{4,5},{5,6},{6,7},{7,0},{8,9},{9,10},{10,1... | collective-permute-start | bytes 3145736 | tf_op jit(solution)/shard_map/while/body/eval_jaxpr/ppermute | solution.py:21
  395.3 5.6 collective-permute-start.3
  401.0 8.2 copy-start.4
  401.0 53.4 %collective-permute-start.4 = (f32[128]{0:T(128)S(1)}, f32[128]{0:T(128)S(1)}, u32[]{:S(2)}, u32[]{:S(2)}) collective-permute-start(f32[128]{0:T(128)S(1)} %copy.223), channel_id=1, source_target_pairs={{0,1},{1,2},{2,3},{3,4},{4,5},{5,6},{6,7},{7,0},{8,9},{9,10},{10,1... | collective-permute-start | bytes 1544 | tf_op jit(solution)/shard_map/while/body/eval_jaxpr/ppermute | solution.py:21
  401.1 58.0 %collective-permute-start.2 = (f32[128,16]{0,1:T(8,128)S(1)}, f32[128,16]{0,1:T(8,128)S(1)}, u32[]{:S(2)}, u32[]{:S(2)}) collective-permute-start(f32[128,16]{0,1:T(8,128)S(1)} %copy.221), channel_id=1, source_target_pairs={{0,1},{1,2},{2,3},{3,4},{4,5},{5,6},{6,7},{7,0},{8,9},{9,10},{10,1... | collective-permute-start | bytes 24584 | tf_op jit(solution)/shard_map/while/body/eval_jaxpr/ppermute | solution.py:21
  402.4 56.8 %collective-permute-start = (bf16[128,2048]{0,1:T(8,128)(2,1)S(1)}, bf16[128,2048]{0,1:T(8,128)(2,1)S(1)}, u32[]{:S(2)}, u32[]{:S(2)}) collective-permute-start(bf16[128,2048]{0,1:T(8,128)(2,1)S(1)} %copy.219), channel_id=1, source_target_pairs={{0,1},{1,2},{2,3},{3,4},{4,5},{5,6},{6,7},{7,0},{8,9},{9,10},{10,1... | collective-permute-start | bytes 1572872 | tf_op jit(solution)/shard_map/while/body/eval_jaxpr/ppermute | solution.py:21
  404.8 54.4 %collective-permute-start.1 = (bf16[128,2048]{0,1:T(8,128)(2,1)}, bf16[128,2048]{0,1:T(8,128)(2,1)}, u32[]{:S(2)}, u32[]{:S(2)}) collective-permute-start(bf16[128,2048]{0,1:T(8,128)(2,1)} %copy.220), channel_id=1, source_target_pairs={{0,1},{1,2},{2,3},{3,4},{4,5},{5,6},{6,7},{7,0},{8,9},{9,10},{10,1... | collective-permute-start | bytes 1572872 | tf_op jit(solution)/shard_map/while/body/eval_jaxpr/ppermute | solution.py:21
  427.4 31.8 %collective-permute-start.5 = (f32[128,2048]{0,1:T(8,128)}, f32[128,2048]{0,1:T(8,128)}, u32[]{:S(2)}, u32[]{:S(2)}) collective-permute-start(f32[128,2048]{0,1:T(8,128)} %bitcast_add_fusion.17), channel_id=1, source_target_pairs={{0,1},{1,2},{2,3},{3,4},{4,5},{5,6},{6,7},{7,0},{8,9},{9,10},{10,1... | collective-permute-start | bytes 3145736 | tf_op jit(solution)/shard_map/while/body/eval_jaxpr/ppermute | solution.py:21
  454.6 4.6 collective-permute-start.3
  459.2 7.3 copy-start.4
  459.3 52.9 %collective-permute-start.4 = (f32[128]{0:T(128)S(1)}, f32[128]{0:T(128)S(1)}, u32[]{:S(2)}, u32[]{:S(2)}) collective-permute-start(f32[128]{0:T(128)S(1)} %copy.223), channel_id=1, source_target_pairs={{0,1},{1,2},{2,3},{3,4},{4,5},{5,6},{6,7},{7,0},{8,9},{9,10},{10,1... | collective-permute-start | bytes 1544 | tf_op jit(solution)/shard_map/while/body/eval_jaxpr/ppermute | solution.py:21
  459.4 59.0 %collective-permute-start.2 = (f32[128,16]{0,1:T(8,128)S(1)}, f32[128,16]{0,1:T(8,128)S(1)}, u32[]{:S(2)}, u32[]{:S(2)}) collective-permute-start(f32[128,16]{0,1:T(8,128)S(1)} %copy.221), channel_id=1, source_target_pairs={{0,1},{1,2},{2,3},{3,4},{4,5},{5,6},{6,7},{7,0},{8,9},{9,10},{10,1... | collective-permute-start | bytes 24584 | tf_op jit(solution)/shard_map/while/body/eval_jaxpr/ppermute | solution.py:21
  461.6 56.8 %collective-permute-start = (bf16[128,2048]{0,1:T(8,128)(2,1)S(1)}, bf16[128,2048]{0,1:T(8,128)(2,1)S(1)}, u32[]{:S(2)}, u32[]{:S(2)}) collective-permute-start(bf16[128,2048]{0,1:T(8,128)(2,1)S(1)} %copy.219), channel_id=1, source_target_pairs={{0,1},{1,2},{2,3},{3,4},{4,5},{5,6},{6,7},{7,0},{8,9},{9,10},{10,1... | collective-permute-start | bytes 1572872 | tf_op jit(solution)/shard_map/while/body/eval_jaxpr/ppermute | solution.py:21
  463.7 54.8 %collective-permute-start.1 = (bf16[128,2048]{0,1:T(8,128)(2,1)}, bf16[128,2048]{0,1:T(8,128)(2,1)}, u32[]{:S(2)}, u32[]{:S(2)}) collective-permute-start(bf16[128,2048]{0,1:T(8,128)(2,1)} %copy.220), channel_id=1, source_target_pairs={{0,1},{1,2},{2,3},{3,4},{4,5},{5,6},{6,7},{7,0},{8,9},{9,10},{10,1... | collective-permute-start | bytes 1572872 | tf_op jit(solution)/shard_map/while/body/eval_jaxpr/ppermute | solution.py:21
  484.8 33.7 %collective-permute-start.5 = (f32[128,2048]{0,1:T(8,128)}, f32[128,2048]{0,1:T(8,128)}, u32[]{:S(2)}, u32[]{:S(2)}) collective-permute-start(f32[128,2048]{0,1:T(8,128)} %bitcast_add_fusion.17), channel_id=1, source_target_pairs={{0,1},{1,2},{2,3},{3,4},{4,5},{5,6},{6,7},{7,0},{8,9},{9,10},{10,1... | collective-permute-start | bytes 3145736 | tf_op jit(solution)/shard_map/while/body/eval_jaxpr/ppermute | solution.py:21
  509.5 5.5 copy-start.11
  512.4 6.1 collective-permute-start.3
  518.5 7.3 copy-start.4
  518.5 52.5 %collective-permute-start.4 = (f32[128]{0:T(128)S(1)}, f32[128]{0:T(128)S(1)}, u32[]{:S(2)}, u32[]{:S(2)}) collective-permute-start(f32[128]{0:T(128)S(1)} %copy.223), channel_id=1, source_target_pairs={{0,1},{1,2},{2,3},{3,4},{4,5},{5,6},{6,7},{7,0},{8,9},{9,10},{10,1... | collective-permute-start | bytes 1544 | tf_op jit(solution)/shard_map/while/body/eval_jaxpr/ppermute | solution.py:21
  518.7 57.1 %collective-permute-start.2 = (f32[128,16]{0,1:T(8,128)S(1)}, f32[128,16]{0,1:T(8,128)S(1)}, u32[]{:S(2)}, u32[]{:S(2)}) collective-permute-start(f32[128,16]{0,1:T(8,128)S(1)} %copy.221), channel_id=1, source_target_pairs={{0,1},{1,2},{2,3},{3,4},{4,5},{5,6},{6,7},{7,0},{8,9},{9,10},{10,1... | collective-permute-start | bytes 24584 | tf_op jit(solution)/shard_map/while/body/eval_jaxpr/ppermute | solution.py:21
  519.9 55.9 %collective-permute-start = (bf16[128,2048]{0,1:T(8,128)(2,1)S(1)}, bf16[128,2048]{0,1:T(8,128)(2,1)S(1)}, u32[]{:S(2)}, u32[]{:S(2)}) collective-permute-start(bf16[128,2048]{0,1:T(8,128)(2,1)S(1)} %copy.219), channel_id=1, source_target_pairs={{0,1},{1,2},{2,3},{3,4},{4,5},{5,6},{6,7},{7,0},{8,9},{9,10},{10,1... | collective-permute-start | bytes 1572872 | tf_op jit(solution)/shard_map/while/body/eval_jaxpr/ppermute | solution.py:21
  521.9 53.9 %collective-permute-start.1 = (bf16[128,2048]{0,1:T(8,128)(2,1)}, bf16[128,2048]{0,1:T(8,128)(2,1)}, u32[]{:S(2)}, u32[]{:S(2)}) collective-permute-start(bf16[128,2048]{0,1:T(8,128)(2,1)} %copy.220), channel_id=1, source_target_pairs={{0,1},{1,2},{2,3},{3,4},{4,5},{5,6},{6,7},{7,0},{8,9},{9,10},{10,1... | collective-permute-start | bytes 1572872 | tf_op jit(solution)/shard_map/while/body/eval_jaxpr/ppermute | solution.py:21
  544.1 31.8 %collective-permute-start.5 = (f32[128,2048]{0,1:T(8,128)}, f32[128,2048]{0,1:T(8,128)}, u32[]{:S(2)}, u32[]{:S(2)}) collective-permute-start(f32[128,2048]{0,1:T(8,128)} %bitcast_add_fusion.17), channel_id=1, source_target_pairs={{0,1},{1,2},{2,3},{3,4},{4,5},{5,6},{6,7},{7,0},{8,9},{9,10},{10,1... | collective-permute-start | bytes 3145736 | tf_op jit(solution)/shard_map/while/body/eval_jaxpr/ppermute | solution.py:21
  571.2 4.6 collective-permute-start.3
  580.7 176.8 %reduce-scatter.3.cloned.1.call-start = ((), (), s32[]{:S(2)}) async-start(), calls=%async_computation.4 | async-start | bytes 4456448 | tf_op jit(solution)/shard_map/reduce_scatter | solution.py:182
  586.2 394.9 %all-reduce.3.cloned.1.call-start = ((), (), s32[]{:S(2)}) async-start(), calls=%async_computation.6 | async-start | bytes 33554432 | tf_op jit(solution)/shard_map/psum | solution.py:188
  (81 other events, 236.4 us)
Sparse Core Ops, SparseCore 0:
  10.9 50.5 all-gather.3
  64.3 45.0 all-gather.5
  580.8 92.3 reduce-scatter.4
  678.2 79.3 reduce-scatter.2
  763.7 217.4 all-reduce.2
where the time goes:
time: 1010 us
  waiting for transfers between devices  448 us (44%)
  matrix products  269 us (27%)
  other arithmetic  126 us (12%)
  local copies, waits for them, and re-layouts  73.6 us (7%)
  starting transfers between devices  47.4 us (5%)
  blocking collectives  25.7 us (3%)
  between operations  13.9 us (1%)
    psum x1, waiting for transfers between devices, local(): grad_wk, grad_wv = lax.psum((term_k, term_v), ('inner', 'outer'))  216 us
    dot_general x32, matrix products, attend(): jnp.einsum('grqk,qgrd->kgd', probs_low, gradient_per_head, preferred_elem...  95.8 us
    add x32, other arithmetic, advance(): sums[piece_index][1] + slice_values  89.8 us
    reduce_scatter x1, waiting for transfers between devices, local(): lax.psum_scatter(sum_values, 'inner', scatter_dimension=0, tiled=True)  86.9 us
    dot_general x32, matrix products, attend(): jnp.einsum('qgrd,kgd->grqk', gradient_per_head, value_per_head, preferred...  81.4 us
    reduce_scatter x1, waiting for transfers between devices, local(): lax.psum_scatter(sum_keys, 'inner', scatter_dimension=0, tiled=True)  78.7 us
    all_gather x1, waiting for transfers between devices, local(): lax.all_gather(values, 'inner', axis=0, tiled=True)  48 us
    ppermute x48, starting transfers between devices, from_behind(): lax.ppermute(value, axis, [(i, (i + by) % length) for i in range(length)])  47.2 us
  transfers between devices with their start and end apart: 53, of which 7 were waited for; matrix products, arithmetic and copies ran while one was open for 42% of the time, Pallas kernels for 0%

commit v1 on v0

v1 whole, which is shorter than its diff:
```python
import functools
import math

import jax
import jax.numpy as jnp
from jax import lax
from jax.experimental import pallas as pl
from jax.experimental.pallas import tpu as pltpu
from jax.sharding import PartitionSpec as P

HEAD = 128
GROUPS = 2
SHARE = 4
RUN = 64
KEYS = 4096
KEY_RUNS = KEYS // RUN
QUERY_ROWS = 1024
QUERY_RUNS = QUERY_ROWS // RUN
UNIT = 2
CHUNK = 512
SCALE = HEAD**-0.5
LOG2E = math.log2(math.e)
F32 = jnp.float32
BF16 = jnp.bfloat16
MESH = pl.DeviceIdType.MESH
NT = (((1,), (1,)), ((), ()))
NN = (((1,), (0,)), ((), ()))
VMEM = pl.BlockSpec(memory_space=pltpu.VMEM)
SMEM = pl.BlockSpec(memory_space=pltpu.SMEM)
HBM = pl.BlockSpec(memory_space=pltpu.HBM)
PARTS = (6, 5, 5)
ORDERS = ("zxy", "xyz", "yzx")


def dot(a, b, dims):
    return lax.dot_general(a, b, dims, preferred_element_type=F32)


def wrap(value):
    return lax.rem(value + 4, 4)


class Place:
    def __init__(self):
        inner, outer = lax.axis_index("inner"), lax.axis_index("outer")
        c = lax.rem(inner, 2)
        x = lax.div(inner, 8) * 2 + lax.div(outer, 4)
        y = lax.rem(lax.div(inner, 2), 4)
        z = lax.rem(outer, 4)
        self.c = c
        self.at = {"x": x, "y": y, "z": z, "L": z + c * (x - z), "M": x + c * (z - x)}
        self.step = {"x": (1, 0, 0), "y": (0, 1, 0), "z": (0, 0, 1), "L": (c, 0, 1 - c), "M": (1 - c, 0, c)}

    def device(self, axis=None, by=0, other=False):
        step = (0, 0, 0) if axis is None else self.step[axis]
        x, y, z = (wrap(self.at[name] + by * d) for name, d in zip("xyz", step))
        c = 1 - self.c if other else self.c
        return ((lax.div(x, 2) * 4 + y) * 2 + c, lax.rem(x, 2) * 4 + z)

    def beside(self):
        near = [self.device(axis, by) for axis in "xyz" for by in (1, -1, 2)]
        return near + [self.device(other=True)]


class Net:
    def __init__(self, place, send_sems, recv_sems):
        self.place, self.send_sems, self.recv_sems = place, send_sems, recv_sems
        self.sent = []

    def greet(self):
        barrier = pltpu.get_barrier_semaphore()
        near = self.place.beside()
        for device in near:
            pl.semaphore_signal(barrier, inc=1, device_id=device, device_id_type=MESH)
        pl.semaphore_wait(barrier, len(near))

    def send(self, src, dst, device):
        k = len(self.sent)
        assert k < self.send_sems.shape[0]
        copy = pltpu.make_async_remote_copy(
            src_ref=src,
            dst_ref=dst,
            send_sem=self.send_sems.at[k],
            recv_sem=self.recv_sems.at[k],
            device_id=device,
            device_id_type=MESH,
        )
        copy.start()
        self.sent.append(copy)
        return copy

    def finish(self):
        for copy in self.sent:
            copy.wait_send()

    def pair(self, axis, src, dst):
        return [self.send(src, dst, self.place.device(axis, by)) for by in (1, -1)]

    def relay(self, axis, pair, ref, n):
        s = self.place.at[axis]
        low, high = pl.ds(0, n // 2), pl.ds(n // 2, n - n // 2)
        pair[0].wait_recv()
        block = ref(wrap(s - 1), low)
        up = self.send(block, block, self.place.device(axis, 1))
        pair[1].wait_recv()
        block = ref(wrap(s + 1), high)
        return [up, self.send(block, block, self.place.device(axis, -1))]

    def cast(self, axis, block):
        return [self.send(block, block, self.place.device(axis, by)) for by in (1, -1, 2)]

    def scatter(self, axis, hbm, buf, relay, from_behind, from_ahead, out):
        s = self.place.at[axis]
        ahead, behind = self.place.device(axis, 1), self.place.device(axis, -1)
        n = buf.shape[1]
        h = n // 2
        low, high = pl.ds(0, h), pl.ds(h, n - h)
        far, left, right = wrap(s + 2), wrap(s - 1), wrap(s + 1)
        relay_up = self.send(hbm.at[far, low], relay.at[low], ahead)
        relay_down = self.send(hbm.at[far, high], relay.at[high], behind)
        up_high = self.send(hbm.at[right, high], from_behind.at[high], ahead)
        down_low = self.send(hbm.at[left, low], from_ahead.at[low], behind)
        yield
        relay_up.wait_recv()
        buf[right, low] = (buf[right, low].astype(F32) + relay[low].astype(F32)).astype(BF16)
        up_low = self.send(buf.at[right, low], from_behind.at[low], ahead)
        relay_down.wait_recv()
        buf[left, high] = (buf[left, high].astype(F32) + relay[high].astype(F32)).astype(BF16)
        down_high = self.send(buf.at[left, high], from_ahead.at[high], behind)
        yield
        for copy in (up_high, down_low, up_low, down_high):
            copy.wait_recv()
        out[...] = (
            buf[s].astype(F32) + from_behind[...].astype(F32) + from_ahead[...].astype(F32)
        ).astype(out.dtype)

    def scatter_direct(self, axis, buf, inbox, out):
        s = self.place.at[axis]
        copies = [
            self.send(buf.at[wrap(s + by)], inbox.at[i], self.place.device(axis, by))
            for i, by in enumerate((1, -1, 2))
        ]
        yield
        for copy in copies:
            copy.wait_recv()
        out[...] = (
            buf[s].astype(F32)
            + inbox[0].astype(F32)
            + inbox[1].astype(F32)
            + inbox[2].astype(F32)
        ).astype(out.dtype)


def together(*chains):
    chains = list(chains)
    while chains:
        for chain in list(chains):
            try:
                next(chain)
            except StopIteration:
                chains.remove(chain)


def gather_kernel(
    q, do, k, v, do_v, ao, lse, pos, qg, dog, kg, vg, sg, pg, stats, mine, spots, send_sems, recv_sems, own_sems
):
    place = Place()
    net = Net(place, send_sems, recv_sems)
    y, c, l, m = place.at["y"], place.c, place.at["L"], place.at["M"]
    twin = place.device(other=True)
    net.greet()
    first, second = (pl.multiple_of(i * 128, 128) for i in (c, 1 - c))

    def cut(columns):
        return [pl.ds(pl.multiple_of(i * columns, columns), columns) for i in (c, 1 - c)]

    wide, thin = cut(1024), cut(256)
    owns = []

    def keep(src, dst):
        copy = pltpu.make_async_copy(src, dst, own_sems.at[len(owns)])
        copy.start()
        owns.append(copy)
        return copy

    def queries_chain(src, buf):
        def block(start):
            return lambda slot, rows: buf.at[slot, pl.ds(start + rows.start, rows.size)]

        whole = pl.ds(0, 128)
        mine_at, twin_at = block(first), block(second)
        from_twin = net.send(src.at[:, wide[1]], buf.at[m, pl.ds(first, 128)], twin)
        pair = net.pair("L", src.at[:, wide[0]], mine_at(l, whole))
        own = keep(src.at[:, wide[0]], mine_at(l, whole))
        yield
        from_twin.wait_recv()
        pair2 = net.pair("L", twin_at(l, whole), twin_at(l, whole))
        yield
        relays = net.relay("L", pair, mine_at, 128)
        yield
        relays += net.relay("L", pair2, twin_at, 128)
        yield
        for copy in relays:
            copy.wait_recv()
        own.wait()

    def keys_chain(src, buf, a, b):
        i, j = place.at[a], place.at[b]
        whole = pl.ds(0, 128)

        def block(start):
            return lambda slot, rows: buf.at[j, slot, pl.ds(start + rows.start, rows.size)]

        def chip(slot):
            return lambda other, rows: buf.at[other, slot, rows]

        def pair_b(slot):
            return (slot, net.pair(b, buf.at[j, slot], buf.at[j, slot]))

        mine_at, twin_at = block(first), block(second)
        there = buf.at[y, l] if a == "M" else buf.at[l, y]
        from_twin = net.send(src.at[:, thin[1]], there.at[pl.ds(first, 128)], twin)
        pair = net.pair(a, src.at[:, thin[0]], mine_at(i, whole))
        own = keep(src.at[:, thin[0]], mine_at(i, whole))
        yield
        from_twin.wait_recv()
        pair2 = net.pair(a, twin_at(i, whole), twin_at(i, whole))
        own.wait()
        pairs = [pair_b(i)]
        yield
        relays = net.relay(a, pair, mine_at, 128)
        yield
        relays += net.relay(a, pair2, twin_at, 128)
        pairs += [pair_b(wrap(i - 1)), pair_b(wrap(i + 1))]
        yield
        for copy in relays:
            copy.wait_recv()
        pairs.append(pair_b(wrap(i + 2)))
        yield
        relays = []
        for slot, both in pairs:
            relays += net.relay(b, both, chip(slot), 256)
        yield
        for copy in relays:
            copy.wait_recv()

    def stats_chain():
        spots[...] = jnp.broadcast_to(pos[...], (8, 128)).astype(F32)
        place_own = keep(spots, pg.at[y, m, c])
        place_twin = net.send(spots, pg.at[y, l, c], twin)
        stats[...] = jnp.zeros_like(stats)
        stats[:, 0:16] = lse[...] * LOG2E
        for h in range(16):
            columns = slice(h * HEAD, (h + 1) * HEAD)
            product = do_v[:, columns].astype(F32) * ao[:, columns].astype(F32)
            stats[:, 16 + h : 17 + h] = jnp.sum(product, axis=1, keepdims=True)
        turned = stats[...].T
        for i in range(2):
            mine[i, 0:8, :] = turned[i * 8 : i * 8 + 8]
            mine[i, 8:16, :] = turned[16 + i * 8 : 24 + i * 8]
            mine[i, 16:24, :] = spots[...]
        stats_twin = net.send(mine.at[1 - c], sg.at[m, c], twin)
        stats_own = keep(mine.at[c], sg.at[l, c])
        yield
        place_own.wait()
        place_twin.wait_recv()
        places = net.cast("M", pg.at[y, m])
        stats_own.wait()
        stats_twin.wait_recv()
        rest = net.cast("L", sg.at[l])
        yield
        for copy in places:
            copy.wait_recv()
        rest += net.cast("y", pg.at[y])
        yield
        yield
        for copy in rest:
            copy.wait_recv()

    together(
        keys_chain(k, kg, "M", "y"),
        keys_chain(v, vg, "y", "M"),
        queries_chain(q, qg),
        queries_chain(do, dog),
        stats_chain(),
    )
    net.finish()


def gather_all(q, do, k, v, ao, lse, pos):
    shape = jax.ShapeDtypeStruct
    return pl.pallas_call(
        gather_kernel,
        out_shape=[
            shape((4, 256, 1024), BF16),
            shape((4, 256, 1024), BF16),
            shape((4, 4, 256, 256), BF16),
            shape((4, 4, 256, 256), BF16),
            shape((4, 2, 24, 128), F32),
            shape((4, 4, 2, 8, 128), F32),
        ],
        in_specs=[HBM] * 4 + [VMEM] * 4,
        out_specs=[HBM] * 6,
        scratch_shapes=[
            pltpu.VMEM((128, 128), F32),
            pltpu.VMEM((2, 24, 128), F32),
            pltpu.VMEM((8, 128), F32),
            pltpu.SemaphoreType.DMA((96,)),
            pltpu.SemaphoreType.DMA((96,)),
            pltpu.SemaphoreType.DMA((6,)),
        ],
        compiler_params=pltpu.CompilerParams(
            collective_id=0, has_side_effects=True, vmem_limit_bytes=60 * 2**20
        ),
    )(q, do, k, v, do, ao, lse, pos)


def attend_kernel(
    rank, order, reach, qplace, kplace, qg, dog, kg, vg, sg, dqp, dkp, dvp,
    q_all, do_all, k_all, v_all, columns, dq_all, dk_all, dv_all,
    qs, dos, qt, dot_, lse_s, delta_s, dq_sum, dk_sum, dv_sum, in_sems, out_sems,
):
    rows = UNIT * SHARE * RUN

    def at_run(ref, j, first):
        a, b, r = lax.div(j, 16), lax.rem(lax.div(j, 4), 4), lax.rem(j, 4)
        part = pl.ds(pl.multiple_of(r * RUN, RUN), RUN)
        return ref.at[a, b, part] if first else ref.at[b, a, part]

    def key_copies(j):
        spot = pl.ds(pl.multiple_of(rank[j] * RUN, RUN), RUN)
        return (
            pltpu.make_async_copy(at_run(kg, j, True), k_all.at[spot], in_sems.at[0]),
            pltpu.make_async_copy(at_run(vg, j, False), v_all.at[spot], in_sems.at[1]),
        )

    def query_copies(r):
        i = order[r]
        part = pl.ds(pl.multiple_of(lax.rem(i, 4) * RUN, RUN), RUN)
        spot = pl.ds(pl.multiple_of(r * RUN, RUN), RUN)
        return (
            pltpu.make_async_copy(qg.at[lax.div(i, 4), part], q_all.at[spot], in_sems.at[2]),
            pltpu.make_async_copy(dog.at[lax.div(i, 4), part], do_all.at[spot], in_sems.at[3]),
        )

    def start(make):
        def body(i, _):
            for copy in make(i):
                copy.start()
            return 0

        return body

    lax.fori_loop(0, QUERY_RUNS, start(query_copies), 0)
    lax.fori_loop(0, KEY_RUNS, start(key_copies), 0)
    for z in range(4):
        for c in range(2):
            spot = (z * 2 + c) * 128
            columns[spot : spot + 128, 0:24] = sg[z, c].T
    dk_sum[...] = jnp.zeros_like(dk_sum)
    dv_sum[...] = jnp.zeros_like(dv_sum)
    pltpu.make_async_copy(q_all, q_all, in_sems.at[2]).wait()
    pltpu.make_async_copy(do_all, do_all, in_sems.at[3]).wait()
    pltpu.make_async_copy(k_all, k_all, in_sems.at[0]).wait()
    pltpu.make_async_copy(v_all, v_all, in_sems.at[1]).wait()

    per = CHUNK // RUN

    def unit(i, _):
        for u in range(UNIT):
            r = i * UNIT + u
            r0 = pl.multiple_of(r * RUN, RUN)
            s0 = pl.multiple_of(order[r] * RUN, RUN)
            for g in range(GROUPS):
                for h in range(SHARE):
                    head = g * SHARE + h
                    o = (u * SHARE + h) * RUN
                    spot = pl.ds(o, RUN)
                    qs[g, spot, :] = q_all[pl.ds(r0, RUN), head * HEAD : (head + 1) * HEAD]
                    dos[g, spot, :] = do_all[pl.ds(r0, RUN), head * HEAD : (head + 1) * HEAD]
                    lse_s[g, spot, :] = columns[pl.ds(s0, RUN), head : head + 1]
                    delta_s[g, spot, :] = columns[pl.ds(s0, RUN), 8 + head : 9 + head]
        for g in range(GROUPS):
            qt[g] = qs[g].T
            dot_[g] = dos[g].T
        dq_sum[...] = jnp.zeros_like(dq_sum)
        first, last = reach[i * UNIT], reach[i * UNIT + UNIT - 1]
        whole, chunks = lax.div(first - 1, per), lax.div(last + per - 1, per)

        def step(masked, chunk, _):
            k0 = pl.multiple_of(chunk * CHUNK, CHUNK)
            keys = pl.ds(k0, CHUNK)
            if masked:
                row = lax.broadcasted_iota(jnp.int32, (rows, 1), 0)
                qpos = lax.rem(row, RUN)
                for u in range(UNIT):
                    inside = lax.div(row, SHARE * RUN) == u
                    qpos = qpos + jnp.where(inside, qplace[i * UNIT + u], 0)
                column = lax.broadcasted_iota(jnp.int32, (1, CHUNK), 1)
                kpos = lax.rem(column, RUN)
                for u in range(per):
                    kpos = kpos + jnp.where(lax.div(column, RUN) == u, kplace[chunk * per + u], 0)
                allowed = kpos <= qpos
            for g in range(GROUPS):
                kk = k_all[keys, g * HEAD : (g + 1) * HEAD]
                vv = v_all[keys, g * HEAD : (g + 1) * HEAD]
                probs = jnp.exp2(dot(qs[g], kk, NT) * (SCALE * LOG2E) - lse_s[g])
                if masked:
                    probs = jnp.where(allowed, probs, 0.0)
                dprobs = dot(dos[g], vv, NT)
                dscores = (probs * (dprobs - delta_s[g])).astype(BF16)
                dq_sum[g] += dot(dscores, kk, NN)
                dv_sum[g, :, keys] += dot(dot_[g], probs.astype(BF16), NN)
                dk_sum[g, :, keys] += dot(qt[g], dscores, NN)
            return 0

        lax.fori_loop(0, whole, functools.partial(step, False), 0)
        lax.fori_loop(whole, chunks, functools.partial(step, True), 0)
        for u in range(UNIT):
            r0 = pl.multiple_of((i * UNIT + u) * RUN, RUN)
            for g in range(GROUPS):
                for h in range(SHARE):
                    head = g * SHARE + h
                    o = (u * SHARE + h) * RUN
                    dq_all[pl.ds(r0, RUN), head * HEAD : (head + 1) * HEAD] = (
                        dq_sum[g, o : o + RUN, :] * SCALE
                    ).astype(BF16)
        return 0

    lax.fori_loop(0, QUERY_RUNS // UNIT, unit, 0)

    def query_back(r):
        i = order[r]
        part = pl.ds(pl.multiple_of(lax.rem(i, 4) * RUN, RUN), RUN)
        spot = pl.ds(pl.multiple_of(r * RUN, RUN), RUN)
        return (pltpu.make_async_copy(dq_all.at[spot], dqp.at[lax.div(i, 4), part], out_sems.at[0]),)

    def key_back(j):
        spot = pl.ds(pl.multiple_of(rank[j] * RUN, RUN), RUN)
        return (
            pltpu.make_async_copy(dk_all.at[spot], at_run(dkp, j, True), out_sems.at[1]),
            pltpu.make_async_copy(dv_all.at[spot], at_run(dvp, j, False), out_sems.at[2]),
        )

    lax.fori_loop(0, QUERY_RUNS, start(query_back), 0)

    def turn(chunk, _):
        keys = pl.ds(pl.multiple_of(chunk * CHUNK, CHUNK), CHUNK)
        for g in range(GROUPS):
            columns_g = slice(g * HEAD, (g + 1) * HEAD)
            dk_all[keys, columns_g] = (dk_sum[g, :, keys] * SCALE).astype(BF16).T
            dv_all[keys, columns_g] = dv_sum[g, :, keys].astype(BF16).T
        return 0

    lax.fori_loop(0, KEYS // CHUNK, turn, 0)
    lax.fori_loop(0, KEY_RUNS, start(key_back), 0)
    pltpu.make_async_copy(dq_all, dq_all, out_sems.at[0]).wait()
    pltpu.make_async_copy(dk_all, dk_all, out_sems.at[1]).wait()
    pltpu.make_async_copy(dv_all, dv_all, out_sems.at[2]).wait()


def attend(rank, order, reach, qplace, kplace, qg, dog, kg, vg, sg):
    shape = jax.ShapeDtypeStruct
    rows = UNIT * SHARE * RUN
    return pl.pallas_call(
        attend_kernel,
        out_shape=[
            shape((4, 256, 1024), BF16),
            shape((4, 4, 256, 256), BF16),
            shape((4, 4, 256, 256), BF16),
        ],
        in_specs=[SMEM] * 5 + [HBM] * 4 + [VMEM],
        out_specs=[HBM] * 3,
        scratch_shapes=[
            pltpu.VMEM((QUERY_ROWS, 1024), BF16),
            pltpu.VMEM((QUERY_ROWS, 1024), BF16),
            pltpu.VMEM((KEYS, 256), BF16),
            pltpu.VMEM((KEYS, 256), BF16),
            pltpu.VMEM((QUERY_ROWS, 24), F32),
            pltpu.VMEM((QUERY_ROWS, 1024), BF16),
            pltpu.VMEM((KEYS, 256), BF16),
            pltpu.VMEM((KEYS, 256), BF16),
            pltpu.VMEM((GROUPS, rows, HEAD), BF16),
            pltpu.VMEM((GROUPS, rows, HEAD), BF16),
            pltpu.VMEM((GROUPS, HEAD, rows), BF16),
            pltpu.VMEM((GROUPS, HEAD, rows), BF16),
            pltpu.VMEM((GROUPS, rows, 1), F32),
            pltpu.VMEM((GROUPS, rows, 1), F32),
            pltpu.VMEM((GROUPS, rows, HEAD), F32),
            pltpu.VMEM((GROUPS, HEAD, KEYS), F32),
            pltpu.VMEM((GROUPS, HEAD, KEYS), F32),
            pltpu.SemaphoreType.DMA((4,)),
            pltpu.SemaphoreType.DMA((3,)),
        ],
        compiler_params=pltpu.CompilerParams(vmem_limit_bytes=60 * 2**20),
    )(rank, order, reach, qplace, kplace, qg, dog, kg, vg, sg)


def reduce_kernel(hidden, dqp, dkp, dvp, dq, *rest):
    wg = rest[0:3]
    (h_twin, ht, dkv, dq_sums, dk_sums, dv_sums) = rest[3:9]
    (dq_relay, dq_up, dq_down, dq_own) = rest[9:13]
    (dk_relay, dk_up, dk_down, dk_mid, dk_inbox) = rest[13:18]
    (dv_relay, dv_up, dv_down, dv_mid, dv_inbox) = rest[18:23]
    spare = rest[23:-3]
    send_sems, recv_sems, own_sems = rest[-3:]
    place = Place()
    net = Net(place, send_sems, recv_sems)
    c = place.c
    twin = place.device(other=True)
    loads = []
    for src, dst in ((dkp, dk_sums), (dvp, dv_sums), (dqp, dq_sums)):
        loads.append(pltpu.make_async_copy(src, dst, own_sems.at[len(loads)]))
        loads[-1].start()
    net.greet()
    rows = pl.ds(pl.multiple_of(c * 128, 128), 128)
    theirs = pl.ds(pl.multiple_of((1 - c) * 128, 128), 128)

    def queries_chain():
        first = net.scatter("L", dqp, dq_sums, dq_relay, dq_up, dq_down, dq_own)
        next(first)
        yield
        loads[2].wait()
        yield from first
        columns = pl.ds(pl.multiple_of(c * 1024, 1024), 1024)
        copy = net.send(dq_own.at[theirs], dq.at[:, columns], twin)
        own = pltpu.make_async_copy(dq_own.at[rows], dq.at[:, columns], own_sems.at[3])
        own.start()
        yield
        own.wait()
        copy.wait_recv()

    def keys_chain(load, hbm, sums, relay, up, down, mid, inbox, a, b, out):
        first = net.scatter(a, hbm, sums, relay, up, down, mid)
        next(first)
        yield
        load.wait()
        yield from first
        yield from net.scatter_direct(b, mid, inbox, out)

    def hidden_chain():
        copy = net.send(hidden, h_twin, twin)
        yield
        copy.wait_recv()
        ht[:, 0:128] = jnp.where(c == 0, hidden[...], h_twin[...]).T
        ht[:, 128:256] = jnp.where(c == 0, h_twin[...], hidden[...]).T

    together(
        keys_chain(
            loads[0], dkp, dk_sums, dk_relay, dk_up, dk_down, dk_mid, dk_inbox, "y", "M", dkv.at[:, 0:256]
        ),
        keys_chain(
            loads[1], dvp, dv_sums, dv_relay, dv_up, dv_down, dv_mid, dv_inbox, "M", "y", dkv.at[:, 256:512]
        ),
        queries_chain(),
        hidden_chain(),
    )

    parts = [spare[i * 10 : (i + 1) * 10] for i in range(3)]
    where = []
    for tile in range(16):
        row, column = tile // 4, tile % 4
        if row < 3:
            where.append((row, column))
        else:
            where.append({0: (1, 4), 1: (2, 4), 2: (0, 4), 3: (0, 5)}[column])

    def project(i, _):
        xi, yi = lax.div(i, 4), lax.rem(i, 4)
        block = pl.ds(pl.multiple_of(i * 256, 256), 256)
        term = dot(ht[block, :], dkv[...], NN).astype(BF16)
        for zi in range(4):
            at = {"x": xi, "y": yi, "z": zi}
            for tile in range(16):
                part, u = where[tile]
                r0, c0 = zi * 64 + (tile // 4) * 16, (tile % 4) * 128
                o = [at[axis] for axis in ORDERS[part]]
                parts[part][0][o[0], o[1], o[2], u] = term[r0 : r0 + 16, c0 : c0 + 128]
        return 0

    lax.fori_loop(0, 16, project, 0)

    def part_chain(p):
        order, whole = ORDERS[p], wg[p]
        terms, relay, up, down, mid, inbox, mid2, inbox2, total = parts[p][:9]
        at = [place.at[axis] for axis in order]
        yield from net.scatter(order[0], terms, terms, relay, up, down, mid)
        yield from net.scatter_direct(order[1], mid, inbox, mid2)
        yield from net.scatter_direct(order[2], mid2, inbox2, total)
        mine = whole.at[c]
        own = pltpu.make_async_copy(total, mine.at[at[0], at[1], at[2]], own_sems.at[4 + p])
        own.start()
        own.wait()
        for copy in net.cast(order[2], mine.at[at[0], at[1], at[2]]):
            yield
            copy.wait_recv()
        for copy in net.cast(order[1], mine.at[at[0], at[1]]):
            yield
            copy.wait_recv()

        def ref(slot, part):
            return mine.at[slot, part]

        def share(slot):
            return net.send(mine.at[slot], mine.at[slot], twin)

        pair = net.pair(order[0], mine.at[at[0]], mine.at[at[0]])
        shares = [share(at[0])]
        yield
        relays = net.relay(order[0], pair, ref, 4)
        shares += [share(wrap(at[0] - 1)), share(wrap(at[0] + 1))]
        yield
        for copy in relays:
            copy.wait_recv()
        shares.append(share(wrap(at[0] + 2)))
        yield
        for copy in shares:
            copy.wait_recv()

    together(*[part_chain(p) for p in range(3)])
    net.finish()


def reduce_all(hidden, dqp, dkp, dvp):
    shape = jax.ShapeDtypeStruct

    def buf(*dims, dtype=BF16):
        return pltpu.VMEM(dims, dtype)

    scratch = [buf(128, 4096), buf(4096, 256), buf(256, 512)]
    scratch += [buf(4, 256, 1024), buf(4, 4, 256, 256), buf(4, 4, 256, 256)]
    scratch += [buf(256, 1024)] * 4
    for _ in range(2):
        scratch += [buf(4, 256, 256)] * 4 + [buf(3, 256, 256)]
    for n in PARTS:
        scratch += [buf(4, 4, 4, n, 16, 128)]
        scratch += [buf(4, 4, n, 16, 128)] * 4 + [buf(3, 4, n, 16, 128)]
        scratch += [buf(4, n, 16, 128, dtype=F32), buf(3, n, 16, 128, dtype=F32)]
        scratch += [buf(n, 16, 128)] * 2
    return pl.pallas_call(
        reduce_kernel,
        out_shape=[shape((128, 2048), BF16)]
        + [shape((2, 4, 4, 4, n, 16, 128), BF16) for n in PARTS],
        in_specs=[VMEM] + [HBM] * 3,
        out_specs=[VMEM] + [HBM] * 3,
        scratch_shapes=scratch
        + [
            pltpu.SemaphoreType.DMA((128,)),
            pltpu.SemaphoreType.DMA((128,)),
            pltpu.SemaphoreType.DMA((8,)),
        ],
        compiler_params=pltpu.CompilerParams(
            collective_id=1, has_side_effects=True, vmem_limit_bytes=60 * 2**20
        ),
    )(hidden, dqp, dkp, dvp)


def widen_kernel(a, b, c, wk, wv):
    for zi in range(4):
        for core in range(2):
            for tile in range(16):
                row, column = tile // 4, tile % 4
                if row == 0:
                    value = a[core, zi, 0, 0, column]
                elif row == 1:
                    value = b[core, 0, 0, zi, column]
                elif row == 2:
                    value = c[core, 0, zi, 0, column]
                elif column == 0:
                    value = b[core, 0, 0, zi, 4]
                elif column == 1:
                    value = c[core, 0, zi, 0, 4]
                else:
                    value = a[core, zi, 0, 0, column + 2]
                r0 = zi * 64 + row * 16
                c0 = core * 256 + (column % 2) * 128
                out = wk if column < 2 else wv
                out[r0 : r0 + 16, c0 : c0 + 128] = value.astype(F32)


def widen(a, b, c):
    shape = jax.ShapeDtypeStruct
    return pl.pallas_call(
        widen_kernel,
        grid=(16,),
        out_shape=[shape((4096, 512), F32)] * 2,
        in_specs=[
            pl.BlockSpec((2, 4, 1, 1, 6, 16, 128), lambda i: (0, 0, i // 4, i % 4, 0, 0, 0)),
            pl.BlockSpec((2, 1, 1, 4, 5, 16, 128), lambda i: (0, i // 4, i % 4, 0, 0, 0, 0)),
            pl.BlockSpec((2, 1, 4, 1, 5, 16, 128), lambda i: (0, i % 4, 0, i // 4, 0, 0, 0)),
        ],
        out_specs=[pl.BlockSpec((256, 512), lambda i: (i, 0))] * 2,
        compiler_params=pltpu.CompilerParams(vmem_limit_bytes=60 * 2**20),
    )(a, b, c)


def local(hidden, q, k, v, ao, do, lse, pos):
    qg, dog, kg, vg, sg, pg = gather_all(q, do, k, v, ao, lse, pos[None, :])
    kp = pg[:, :, :, 0, ::RUN].reshape(KEY_RUNS).astype(jnp.int32)
    qp = sg[:, :, 16, ::RUN].reshape(QUERY_RUNS).astype(jnp.int32)
    rank = jnp.sum(kp[None, :] < kp[:, None], axis=1, dtype=jnp.int32)
    kplace = jnp.sum(
        jnp.where(rank[None, :] == jnp.arange(KEY_RUNS)[:, None], kp[None, :], 0), axis=1, dtype=jnp.int32
    )
    qrank = jnp.sum(qp[None, :] < qp[:, None], axis=1, dtype=jnp.int32)
    here = qrank[None, :] == jnp.arange(QUERY_RUNS)[:, None]
    order = jnp.sum(jnp.where(here, jnp.arange(QUERY_RUNS)[None, :], 0), axis=1, dtype=jnp.int32)
    qplace = jnp.sum(jnp.where(here, qp[None, :], 0), axis=1, dtype=jnp.int32)
    reach = jnp.sum(kp[None, :] <= qplace[:, None], axis=1, dtype=jnp.int32)
    dqp, dkp, dvp = attend(rank, order, reach, qplace, kplace, qg, dog, kg, vg, sg)
    dq, a, b, c = reduce_all(hidden, dqp, dkp, dvp)
    wk, wv = widen(a, b, c)
    return dq, wk, wv


def solution(mesh):
    rows = P(("inner", "outer"), None)
    return jax.shard_map(
        local,
        mesh=mesh,
        in_specs=(rows,) * 7 + (P(("inner", "outer")),),
        out_specs=(rows, P(), P()),
        check_vma=False,
    )
```

time: 1010 us -> 242 us (0.24)
  waiting for transfers between devices: 448 us -> 0 us
  matrix products: 269 us -> 0 us
  Pallas kernels: 0 us -> 228 us
  other arithmetic: 126 us -> 2.41 us
  local copies, waits for them, and re-layouts: 73.6 us -> 10.4 us
  starting transfers between devices: 47.4 us -> 0 us
  blocking collectives: 25.7 us -> 0 us
  between operations: 13.9 us -> 0.68 us
    dot_general x162 -> x0, matrix products: 269 us -> none  [the longest x32 95.8 us: attend(): jnp.einsum('grqk,qgrd->kgd', probs_low, gradient_per_head, preferred_elem...]
    pallas_call x0 -> x4, Pallas kernels: none -> 228 us  [the longest x1 114 us: reduce_all(): pl.pallas_call(reduce_kernel, out_shape=[shape((128, 2048), BF16)] + [sha...]
    psum x1 -> x0, waiting for transfers between devices: 216 us -> none  [local(): grad_wk, grad_wv = lax.psum((term_k, term_v), ('inner', 'outer'))]
    reduce_scatter x2 -> x0, waiting for transfers between devices: 166 us -> none  [the longest x1 86.9 us: local(): lax.psum_scatter(sum_values, 'inner', scatter_dimension=0, tiled=True)]
    add x40 -> x0, other arithmetic: 111 us -> none  [the longest x32 89.8 us: advance(): sums[piece_index][1] + slice_values]
    all_gather x2 -> x0, waiting for transfers between devices: 63.6 us -> none  [the longest x1 48 us: local(): lax.all_gather(values, 'inner', axis=0, tiled=True)]
    ppermute x48 -> x0, starting transfers between devices: 47.2 us -> none  [from_behind(): lax.ppermute(value, axis, [(i, (i + by) % length) for i in range(length)])]
    while x217 -> x0, local copies, waits for them, and re-layouts: 29.6 us -> none
  transfers between devices with their start and end apart: 53 -> 0, of which waited for: 7 -> 0; matrix products, arithmetic and copies ran while one was open for 42% -> 0% of each run, Pallas kernels for 0% -> 0%
where the time goes in v1:
time: 242 us; the launch traced here: 241 us
  Pallas kernels  228 us (94%)
  local copies, waits for them, and re-layouts  10.4 us (4%)
    pallas_call x1, Pallas kernels, reduce_all(): pl.pallas_call(reduce_kernel, out_shape=[shape((128, 2048), BF16)] + [sha...  114 us
    pallas_call x1, Pallas kernels, attend(): pl.pallas_call(attend_kernel, out_shape=[shape((4, 256, 1024), BF16), sha...  55.9 us
    pallas_call x1, Pallas kernels, gather_all(): pl.pallas_call(gather_kernel, out_shape=[shape((4, 256, 1024), BF16), sha...  44.2 us
    pallas_call x1, Pallas kernels, widen(): pl.pallas_call(widen_kernel, grid=(16,), out_shape=[shape((4096, 512), F3...  13.6 us
    slice x1, local copies, waits for them, and re-layouts, local(): kp = pg[:, :, :, 0, ::RUN].reshape(KEY_RUNS).astype(jnp.int32)  6.31 us

profile of v1, /device:TPU:1, one launch (start us, length us, event | category | flops | bytes accessed | tf_op | source)
XLA Modules:
  0.0 241.1 jit_solution(13973585093100654869)
XLA Ops:
  0.6 1.4 copy.13.lse
  2.1 44.2 %shard_map.103 = (bf16[4,256,1024]{2,1,0:T(8,128)(2,1)}, bf16[4,256,1024]{2,1,0:T(8,128)(2,1)}, bf16[4,4,256,256]{3,2,1,0:T(8,128)(2,1)}, bf16[4,4,256,256]{3,2,...) custom-call(bf16[128,2048]{1,0:T(8,128)(2,1)} %q.1, bf16[128,2048]{1,0:T(8,128)(2,1)} %do_v.1, ...), custom_call_target="tpu_custom_call" | custom-call | tf_op jit(solution)/shard_map/pallas_call | solution.py:292
  46.3 6.3 %slice.6 = f32[4,4,2,1,2]{4,3,2,1,0:T(1,128)S(1)} slice(f32[4,4,2,8,128]{4,3,2,1,0:T(8,128)} %get-tuple-element.18), slice={[0:4:1], [0:4:1], [0:2:1], [0:1:1], [0:128:64]} | slice | bytes 512 | tf_op jit(solution)/shard_map/slice | solution.py:699
  52.6 0.1 convert_reduce_fusion.1
  52.6 0.1 convert_element_type.38
  52.8 0.2 convert_reduce_fusion.rank
  52.9 0.0 copy-start.2
  53.0 0.6 select_reduce_fusion.kplace
  53.6 1.6 slice.7
  55.3 0.1 convert_element_type.41
  55.3 0.2 convert_reduce_fusion.3
  55.5 0.6 select_reduce_fusion.1
  56.2 0.0 copy-start.1
  56.2 0.7 convert_reduce_fusion.2.reach
  56.9 0.0 copy-done.2
  56.9 0.0 copy-done.1
  56.9 55.9 %shard_map.104 = (bf16[4,256,1024]{2,1,0:T(8,128)(2,1)}, bf16[4,4,256,256]{3,2,1,0:T(8,128)(2,1)}, bf16[4,4,256,256]{3,2,1,0:T(8,128)(2,1)}) custom-call(s32[64]{0:T(128)} %copy-done.2, s32[16]{0:T(128)} %get-tuple-element.34.order, s32[16]{0:T(128)} %convert_reduce_fusion.2.reach, s32[16]{0:T(128)} %copy-done.1, s32[64]{0:T(128)} %select_reduce_fusion.kplace, ...), custom_call_target="tpu_custom_call" | custom-call | tf_op jit(solution)/shard_map/pallas_call | solution.py:465
  112.7 113.9 %shard_map.105 = (bf16[128,2048]{1,0:T(8,128)(2,1)}, bf16[2,4,4,4,6,16,128]{6,5,4,3,2,1,0:T(8,128)(2,1)}, bf16[2,4,4,4,5,16,128]{6,5,4,3,2,1,0:T(8,128)(2,1)}, bf16[2,4,4,4,5,16,128]{6,5,4,3,2,1,0:T(8,128)(2,1)}) custom-call(bf16[128,4096]{1,0:T(8,128)(2,1)} %hidden.1, bf16[4,256,1024]{2,1,0:T(8,128)(2,1)} %get-tuple-element.24.dqp, ...), custom_call_target="tpu_custom_call" | custom-call | tf_op jit(solution)/shard_map/pallas_call | solution.py:640
  226.6 0.0 copy-start
  226.6 13.6 %shard_map.106 = (f32[4096,512]{1,0:T(8,128)}, f32[4096,512]{1,0:T(8,128)}) custom-call(bf16[2,4,4,4,6,16,128]{6,5,4,3,2,1,0:T(8,128)(2,1)} %get-tuple-element.28.a, bf16[2,4,4,4,5,16,128]{6,5,4,3,2,1,0:T(8,128)(2,1)} %get-tuple-element.29.b, bf16[2,4,4,4,5,16,128]{6,5,4,3,2,1,0:T(8,128)(2,1)} %get-tuple-element.30.c), custom_call_target="tpu_custom_call" | custom-call | tf_op jit(solution)/shard_map/pallas_call | solution.py:683
  240.3 0.0 copy-done
  240.3 0.8 copy.15
  (1 shorter events, 0.0 us)
Async XLA Ops:
  52.9 3.9 %copy-start.2 = (s32[64]{0:T(128)}, s32[64]{0:T(128)S(1)}, u32[]{:S(2)}) copy-start(s32[64]{0:T(128)S(1)} %convert_reduce_fusion.rank) | copy-start | bytes 772
  56.2 0.7 copy-start.1
  226.6 13.7 %copy-start = (bf16[128,2048]{1,0:T(8,128)(2,1)S(1)}, bf16[128,2048]{1,0:T(8,128)(2,1)}, u32[]{:S(2)}) copy-start(bf16[128,2048]{1,0:T(8,128)(2,1)} %get-tuple-element.38) | copy-start | bytes 1572868

commit v2 on v1

--- a/solution.py
+++ b/solution.py
@@ -28,8 +28,12 @@
 VMEM = pl.BlockSpec(memory_space=pltpu.VMEM)
 SMEM = pl.BlockSpec(memory_space=pltpu.SMEM)
 HBM = pl.BlockSpec(memory_space=pltpu.HBM)
-PARTS = (6, 5, 5)
 ORDERS = ("zxy", "xyz", "yzx")
+PARTS = (
+    (((0, 0), (0, 1), (3, 0)), ((1, 0), (1, 1), (3, 1)), ((2, 0), (2, 1))),
+    (((0, 0), (0, 1), (3, 0)), ((1, 0), (1, 1)), ((2, 0), (2, 1), (3, 1))),
+)
+SIZES = [len(tiles) for batch in PARTS for tiles in batch]
 
 
 def dot(a, b, dims):
@@ -109,29 +113,30 @@
     def cast(self, axis, block):
         return [self.send(block, block, self.place.device(axis, by)) for by in (1, -1, 2)]
 
-    def scatter(self, axis, hbm, buf, relay, from_behind, from_ahead, out):
+    def scatter(self, axis, hbm, buf, at, n, relay, from_behind, from_ahead, out):
         s = self.place.at[axis]
         ahead, behind = self.place.device(axis, 1), self.place.device(axis, -1)
-        n = buf.shape[1]
         h = n // 2
-        low, high = pl.ds(0, h), pl.ds(h, n - h)
+        low, high, whole = pl.ds(0, h), pl.ds(h, n - h), pl.ds(0, n)
         far, left, right = wrap(s + 2), wrap(s - 1), wrap(s + 1)
-        relay_up = self.send(hbm.at[far, low], relay.at[low], ahead)
-        relay_down = self.send(hbm.at[far, high], relay.at[high], behind)
-        up_high = self.send(hbm.at[right, high], from_behind.at[high], ahead)
-        down_low = self.send(hbm.at[left, low], from_ahead.at[low], behind)
+        relay_up = self.send(hbm.at[at(far, low)], relay.at[low], ahead)
+        relay_down = self.send(hbm.at[at(far, high)], relay.at[high], behind)
+        up_high = self.send(hbm.at[at(right, high)], from_behind.at[high], ahead)
+        down_low = self.send(hbm.at[at(left, low)], from_ahead.at[low], behind)
         yield
         relay_up.wait_recv()
-        buf[right, low] = (buf[right, low].astype(F32) + relay[low].astype(F32)).astype(BF16)
-        up_low = self.send(buf.at[right, low], from_behind.at[low], ahead)
+        spot = at(right, low)
+        buf[spot] = (buf[spot].astype(F32) + relay[low].astype(F32)).astype(BF16)
+        up_low = self.send(buf.at[spot], from_behind.at[low], ahead)
         relay_down.wait_recv()
-        buf[left, high] = (buf[left, high].astype(F32) + relay[high].astype(F32)).astype(BF16)
-        down_high = self.send(buf.at[left, high], from_ahead.at[high], behind)
+        spot = at(left, high)
+        buf[spot] = (buf[spot].astype(F32) + relay[high].astype(F32)).astype(BF16)
+        down_high = self.send(buf.at[spot], from_ahead.at[high], behind)
         yield
         for copy in (up_high, down_low, up_low, down_high):
             copy.wait_recv()
         out[...] = (
-            buf[s].astype(F32) + from_behind[...].astype(F32) + from_ahead[...].astype(F32)
+            buf[at(s, whole)].astype(F32) + from_behind[...].astype(F32) + from_ahead[...].astype(F32)
         ).astype(out.dtype)
 
     def scatter_direct(self, axis, buf, inbox, out):
@@ -162,7 +167,7 @@
 
 
 def gather_kernel(
-    q, do, k, v, do_v, ao, lse, pos, qg, dog, kg, vg, sg, pg, stats, mine, spots, send_sems, recv_sems, own_sems
+    q, do, k, v, do_v, ao, lse, pos, qg, dog, kg, vg, sg, pq, pk, stats, mine, send_sems, recv_sems, own_sems
 ):
     place = Place()
     net = Net(place, send_sems, recv_sems)
@@ -245,33 +250,29 @@
             copy.wait_recv()
 
     def stats_chain():
-        spots[...] = jnp.broadcast_to(pos[...], (8, 128)).astype(F32)
-        place_own = keep(spots, pg.at[y, m, c])
-        place_twin = net.send(spots, pg.at[y, l, c], twin)
-        stats[...] = jnp.zeros_like(stats)
-        stats[:, 0:16] = lse[...] * LOG2E
+        kept = [keep(pos, pk.at[y, m, c]), keep(pos, pq.at[l, c])]
+        from_twin = [net.send(pos, pk.at[y, l, c], twin), net.send(pos, pq.at[m, c], twin)]
         for h in range(16):
             columns = slice(h * HEAD, (h + 1) * HEAD)
             product = do_v[:, columns].astype(F32) * ao[:, columns].astype(F32)
-            stats[:, 16 + h : 17 + h] = jnp.sum(product, axis=1, keepdims=True)
+            stats[:, h : h + 1] = jnp.sum(product, axis=1, keepdims=True)
         turned = stats[...].T
         for i in range(2):
-            mine[i, 0:8, :] = turned[i * 8 : i * 8 + 8]
-            mine[i, 8:16, :] = turned[16 + i * 8 : 24 + i * 8]
-            mine[i, 16:24, :] = spots[...]
-        stats_twin = net.send(mine.at[1 - c], sg.at[m, c], twin)
-        stats_own = keep(mine.at[c], sg.at[l, c])
-        yield
-        place_own.wait()
-        place_twin.wait_recv()
-        places = net.cast("M", pg.at[y, m])
-        stats_own.wait()
-        stats_twin.wait_recv()
-        rest = net.cast("L", sg.at[l])
+            mine[i, 0:8, :] = lse[i * 8 : i * 8 + 8] * LOG2E
+            mine[i, 8:16, :] = turned[i * 8 : i * 8 + 8]
+        from_twin.append(net.send(mine.at[1 - c], sg.at[m, c], twin))
+        kept.append(keep(mine.at[c], sg.at[l, c]))
+        yield
+        for copy in kept:
+            copy.wait()
+        for copy in from_twin:
+            copy.wait_recv()
+        places = net.cast("M", pk.at[y, m])
+        rest = net.cast("L", sg.at[l]) + net.cast("L", pq.at[l])
         yield
         for copy in places:
             copy.wait_recv()
-        rest += net.cast("y", pg.at[y])
+        rest += net.cast("y", pk.at[y])
         yield
         yield
         for copy in rest:
@@ -296,18 +297,18 @@
             shape((4, 256, 1024), BF16),
             shape((4, 4, 256, 256), BF16),
             shape((4, 4, 256, 256), BF16),
-            shape((4, 2, 24, 128), F32),
-            shape((4, 4, 2, 8, 128), F32),
+            shape((4, 2, 16, 128), F32),
+            shape((4, 2, 1, 128), jnp.int32),
+            shape((4, 4, 2, 1, 128), jnp.int32),
         ],
         in_specs=[HBM] * 4 + [VMEM] * 4,
-        out_specs=[HBM] * 6,
+        out_specs=[HBM] * 7,
         scratch_shapes=[
             pltpu.VMEM((128, 128), F32),
-            pltpu.VMEM((2, 24, 128), F32),
-            pltpu.VMEM((8, 128), F32),
+            pltpu.VMEM((2, 16, 128), F32),
             pltpu.SemaphoreType.DMA((96,)),
             pltpu.SemaphoreType.DMA((96,)),
-            pltpu.SemaphoreType.DMA((6,)),
+            pltpu.SemaphoreType.DMA((8,)),
         ],
         compiler_params=pltpu.CompilerParams(
             collective_id=0, has_side_effects=True, vmem_limit_bytes=60 * 2**20
@@ -316,7 +317,7 @@
 
 
 def attend_kernel(
-    rank, order, reach, qplace, kplace, qg, dog, kg, vg, sg, dqp, dkp, dvp,
+    pq, pk, qg, dog, kg, vg, sg, dqp, dkp, dvp, order, reach, qplace, rank, kplace, found, found_s,
     q_all, do_all, k_all, v_all, columns, dq_all, dk_all, dv_all,
     qs, dos, qt, dot_, lse_s, delta_s, dq_sum, dk_sum, dv_sum, in_sems, out_sems,
 ):
@@ -351,12 +352,60 @@
 
         return body
 
-    lax.fori_loop(0, QUERY_RUNS, start(query_copies), 0)
-    lax.fori_loop(0, KEY_RUNS, start(key_copies), 0)
+    def query_place(i):
+        return pq[lax.div(i, 4), lax.rem(lax.div(i, 2), 2), 0, lax.rem(i, 2) * RUN]
+
+    def key_place(j):
+        c = lax.rem(lax.div(j, 2), 2)
+        return pk[lax.div(j, 16), lax.rem(lax.div(j, 4), 4), c, 0, lax.rem(j, 2) * RUN]
+
+    lane = lax.broadcasted_iota(jnp.int32, (1, 128), 1)
+    blank = jnp.zeros((1, 128), jnp.int32)
+    query_row = lax.fori_loop(
+        0, QUERY_RUNS, lambda i, row: jnp.where(lane == i, query_place(i), row), blank, unroll=True
+    )
+    key_row = lax.fori_loop(
+        0, KEY_RUNS, lambda j, row: jnp.where(lane == j, key_place(j), row), blank, unroll=True
+    )
+
+    def count_queries(i, total):
+        return total + jnp.where(query_place(i) < query_row, 1, 0)
+
+    def count_keys(j, totals):
+        place = key_place(j)
+        return (
+            totals[0] + jnp.where(place < key_row, 1, 0),
+            totals[1] + jnp.where(place <= query_row, 1, 0),
+        )
+
+    found[0:1, :] = lax.fori_loop(0, QUERY_RUNS, count_queries, blank, unroll=True)
+    key_rank, query_reach = lax.fori_loop(0, KEY_RUNS, count_keys, (blank, blank), unroll=True)
+    found[1:2, :] = query_reach
+    found[2:3, :] = key_rank
+    copy = pltpu.make_async_copy(found, found_s, in_sems.at[4])
+    copy.start()
     for z in range(4):
         for c in range(2):
             spot = (z * 2 + c) * 128
-            columns[spot : spot + 128, 0:24] = sg[z, c].T
+            columns[spot : spot + 128, 0:16] = sg[z, c].T
+    copy.wait()
+
+    def place_query(i, _):
+        r = found_s[0, i]
+        order[r] = i
+        reach[r] = found_s[1, i]
+        qplace[r] = query_place(i)
+        return 0
+
+    def place_key(j, _):
+        rank[j] = found_s[2, j]
+        kplace[found_s[2, j]] = key_place(j)
+        return 0
+
+    lax.fori_loop(0, QUERY_RUNS, place_query, 0)
+    lax.fori_loop(0, QUERY_RUNS, start(query_copies), 0)
+    lax.fori_loop(0, KEY_RUNS, place_key, 0)
+    lax.fori_loop(0, KEY_RUNS, start(key_copies), 0)
     dk_sum[...] = jnp.zeros_like(dk_sum)
     dv_sum[...] = jnp.zeros_like(dv_sum)
     pltpu.make_async_copy(q_all, q_all, in_sems.at[2]).wait()
@@ -459,7 +508,7 @@
     pltpu.make_async_copy(dv_all, dv_all, out_sems.at[2]).wait()
 
 
-def attend(rank, order, reach, qplace, kplace, qg, dog, kg, vg, sg):
+def attend(pq, pk, qg, dog, kg, vg, sg):
     shape = jax.ShapeDtypeStruct
     rows = UNIT * SHARE * RUN
     return pl.pallas_call(
@@ -469,14 +518,21 @@
             shape((4, 4, 256, 256), BF16),
             shape((4, 4, 256, 256), BF16),
         ],
-        in_specs=[SMEM] * 5 + [HBM] * 4 + [VMEM],
+        in_specs=[SMEM] * 2 + [HBM] * 4 + [VMEM],
         out_specs=[HBM] * 3,
         scratch_shapes=[
+            pltpu.SMEM((QUERY_RUNS,), jnp.int32),
+            pltpu.SMEM((QUERY_RUNS,), jnp.int32),
+            pltpu.SMEM((QUERY_RUNS,), jnp.int32),
+            pltpu.SMEM((KEY_RUNS,), jnp.int32),
+            pltpu.SMEM((KEY_RUNS,), jnp.int32),
+            pltpu.VMEM((8, 128), jnp.int32),
+            pltpu.SMEM((8, 128), jnp.int32),
             pltpu.VMEM((QUERY_ROWS, 1024), BF16),
             pltpu.VMEM((QUERY_ROWS, 1024), BF16),
             pltpu.VMEM((KEYS, 256), BF16),
             pltpu.VMEM((KEYS, 256), BF16),
-            pltpu.VMEM((QUERY_ROWS, 24), F32),
+            pltpu.VMEM((QUERY_ROWS, 16), F32),
             pltpu.VMEM((QUERY_ROWS, 1024), BF16),
             pltpu.VMEM((KEYS, 256), BF16),
             pltpu.VMEM((KEYS, 256), BF16),
@@ -489,21 +545,26 @@
             pltpu.VMEM((GROUPS, rows, HEAD), F32),
             pltpu.VMEM((GROUPS, HEAD, KEYS), F32),
             pltpu.VMEM((GROUPS, HEAD, KEYS), F32),
-            pltpu.SemaphoreType.DMA((4,)),
+            pltpu.SemaphoreType.DMA((5,)),
             pltpu.SemaphoreType.DMA((3,)),
         ],
         compiler_params=pltpu.CompilerParams(vmem_limit_bytes=60 * 2**20),
-    )(rank, order, reach, qplace, kplace, qg, dog, kg, vg, sg)
+    )(pq, pk, qg, dog, kg, vg, sg)
 
 
 def reduce_kernel(hidden, dqp, dkp, dvp, dq, *rest):
-    wg = rest[0:3]
-    (h_twin, ht, dkv, dq_sums, dk_sums, dv_sums) = rest[3:9]
-    (dq_relay, dq_up, dq_down, dq_own) = rest[9:13]
-    (dk_relay, dk_up, dk_down, dk_mid, dk_inbox) = rest[13:18]
-    (dv_relay, dv_up, dv_down, dv_mid, dv_inbox) = rest[18:23]
-    spare = rest[23:-3]
-    send_sems, recv_sems, own_sems = rest[-3:]
+    rest = list(rest)
+
+    def take(n):
+        taken, rest[:n] = rest[:n], []
+        return taken
+
+    wg = take(6)
+    h_twin, ht, dkv, dq_sums, dk_sums, dv_sums = take(6)
+    dq_bufs, dq_own = take(3), take(1)[0]
+    term_bufs = [take(5) for _ in range(4)]
+    part_bufs = [take(9) for _ in range(6)]
+    send_sems, recv_sems, own_sems = rest
     place = Place()
     net = Net(place, send_sems, recv_sems)
     c = place.c
@@ -515,12 +576,20 @@
     net.greet()
     rows = pl.ds(pl.multiple_of(c * 128, 128), 128)
     theirs = pl.ds(pl.multiple_of((1 - c) * 128, 128), 128)
+    done = set()
+
+    def loaded(i):
+        if i not in done:
+            loads[i].wait()
+            done.add(i)
 
     def queries_chain():
-        first = net.scatter("L", dqp, dq_sums, dq_relay, dq_up, dq_down, dq_own)
+        for _ in range(3):
+            yield
+        first = net.scatter("L", dqp, dq_sums, lambda slot, part: (slot, part), 256, *dq_bufs, dq_own)
         next(first)
         yield
-        loads[2].wait()
+        loaded(2)
         yield from first
         columns = pl.ds(pl.multiple_of(c * 1024, 1024), 1024)
         copy = net.send(dq_own.at[theirs], dq.at[:, columns], twin)
@@ -530,13 +599,25 @@
         own.wait()
         copy.wait_recv()
 
-    def keys_chain(load, hbm, sums, relay, up, down, mid, inbox, a, b, out):
-        first = net.scatter(a, hbm, sums, relay, up, down, mid)
+    def terms_chain(batch, g):
+        for _ in range(batch):
+            yield
+        hbm, sums = ((dkp, dk_sums), (dvp, dv_sums))[batch]
+        relay, up, down, mid, inbox = term_bufs[batch * 2 + g]
+        axes = ("y", "M") if g == 0 else ("M", "y")
+        columns = pl.ds(g * HEAD, HEAD)
+
+        def at(slot, part):
+            return (slot, part) + (slice(None), columns) if batch == g else (part, slot) + (slice(None), columns)
+
+        first = net.scatter(axes[0], hbm, sums, at, 4, relay, up, down, mid)
         next(first)
         yield
-        load.wait()
+        loaded(batch)
         yield from first
-        yield from net.scatter_direct(b, mid, inbox, out)
+        out = dkv.at[:, pl.ds(batch * 256 + g * HEAD, HEAD)]
+        yield from net.scatter_direct(axes[1], mid, inbox, out)
+        done.add(("terms", batch, g))
 
     def hidden_chain():
         copy = net.send(hidden, h_twin, twin)
@@ -544,58 +625,50 @@
         copy.wait_recv()
         ht[:, 0:128] = jnp.where(c == 0, hidden[...], h_twin[...]).T
         ht[:, 128:256] = jnp.where(c == 0, h_twin[...], hidden[...]).T
-
-    together(
-        keys_chain(
-            loads[0], dkp, dk_sums, dk_relay, dk_up, dk_down, dk_mid, dk_inbox, "y", "M", dkv.at[:, 0:256]
-        ),
-        keys_chain(
-            loads[1], dvp, dv_sums, dv_relay, dv_up, dv_down, dv_mid, dv_inbox, "M", "y", dkv.at[:, 256:512]
-        ),
-        queries_chain(),
-        hidden_chain(),
-    )
-
-    parts = [spare[i * 10 : (i + 1) * 10] for i in range(3)]
-    where = []
-    for tile in range(16):
-        row, column = tile // 4, tile % 4
-        if row < 3:
-            where.append((row, column))
-        else:
-            where.append({0: (1, 4), 1: (2, 4), 2: (0, 4), 3: (0, 5)}[column])
-
-    def project(i, _):
-        xi, yi = lax.div(i, 4), lax.rem(i, 4)
-        block = pl.ds(pl.multiple_of(i * 256, 256), 256)
-        term = dot(ht[block, :], dkv[...], NN).astype(BF16)
-        for zi in range(4):
-            at = {"x": xi, "y": yi, "z": zi}
-            for tile in range(16):
-                part, u = where[tile]
-                r0, c0 = zi * 64 + (tile // 4) * 16, (tile % 4) * 128
-                o = [at[axis] for axis in ORDERS[part]]
-                parts[part][0][o[0], o[1], o[2], u] = term[r0 : r0 + 16, c0 : c0 + 128]
-        return 0
-
-    lax.fori_loop(0, 16, project, 0)
-
-    def part_chain(p):
-        order, whole = ORDERS[p], wg[p]
-        terms, relay, up, down, mid, inbox, mid2, inbox2, total = parts[p][:9]
+        done.add("hidden")
+
+    def project_chain(batch):
+        while not {("terms", batch, 0), ("terms", batch, 1), "hidden"} <= done:
+            yield
+
+        def project(i, _):
+            xi, yi = lax.div(i, 4), lax.rem(i, 4)
+            block = pl.ds(pl.multiple_of(i * 256, 256), 256)
+            term = dot(ht[block, :], dkv[:, batch * 256 : batch * 256 + 256], NN).astype(BF16)
+            for zi in range(4):
+                at = {"x": xi, "y": yi, "z": zi}
+                for p, tiles in enumerate(PARTS[batch]):
+                    o = [at[axis] for axis in ORDERS[p]]
+                    for u, (row, column) in enumerate(tiles):
+                        r0, c0 = zi * 64 + row * 16, column * 128
+                        part_bufs[batch * 3 + p][0][o[0], o[1], o[2], u] = term[r0 : r0 + 16, c0 : c0 + 128]
+            return 0
+
+        lax.fori_loop(0, 16, project, 0)
+        done.add(("project", batch))
+
+    def part_chain(batch, p):
+        while ("project", batch) not in done:
+            yield
+        order, whole = ORDERS[p], wg[batch * 3 + p]
+        terms, relay, up, down, mid, inbox, mid2, inbox2, total = part_bufs[batch * 3 + p]
         at = [place.at[axis] for axis in order]
-        yield from net.scatter(order[0], terms, terms, relay, up, down, mid)
+        yield from net.scatter(
+            order[0], terms, terms, lambda slot, part: (slot, part), 4, relay, up, down, mid
+        )
         yield from net.scatter_direct(order[1], mid, inbox, mid2)
         yield from net.scatter_direct(order[2], mid2, inbox2, total)
         mine = whole.at[c]
-        own = pltpu.make_async_copy(total, mine.at[at[0], at[1], at[2]], own_sems.at[4 + p])
+        own = pltpu.make_async_copy(total, mine.at[at[0], at[1], at[2]], own_sems.at[4 + batch * 3 + p])
         own.start()
         own.wait()
-        for copy in net.cast(order[2], mine.at[at[0], at[1], at[2]]):
-            yield
-            copy.wait_recv()
-        for copy in net.cast(order[1], mine.at[at[0], at[1]]):
-            yield
+        copies = net.cast(order[2], mine.at[at[0], at[1], at[2]])
+        yield
+        for copy in copies:
+            copy.wait_recv()
+        copies = net.cast(order[1], mine.at[at[0], at[1]])
+        yield
+        for copy in copies:
             copy.wait_recv()
 
         def ref(slot, part):
@@ -617,7 +690,12 @@
         for copy in shares:
             copy.wait_recv()
 
-    together(*[part_chain(p) for p in range(3)])
+    chains = []
+    for batch in range(2):
+        chains += [terms_chain(batch, 0), terms_chain(batch, 1)]
+        chains += [hidden_chain()] if batch == 0 else []
+        chains += [project_chain(batch)] + [part_chain(batch, p) for p in range(3)]
+    together(*chains, queries_chain())
     net.finish()
 
 
@@ -630,24 +708,24 @@
     scratch = [buf(128, 4096), buf(4096, 256), buf(256, 512)]
     scratch += [buf(4, 256, 1024), buf(4, 4, 256, 256), buf(4, 4, 256, 256)]
     scratch += [buf(256, 1024)] * 4
-    for _ in range(2):
-        scratch += [buf(4, 256, 256)] * 4 + [buf(3, 256, 256)]
-    for n in PARTS:
+    for _ in range(4):
+        scratch += [buf(4, 256, HEAD)] * 4 + [buf(3, 256, HEAD)]
+    for n in SIZES:
         scratch += [buf(4, 4, 4, n, 16, 128)]
         scratch += [buf(4, 4, n, 16, 128)] * 4 + [buf(3, 4, n, 16, 128)]
         scratch += [buf(4, n, 16, 128, dtype=F32), buf(3, n, 16, 128, dtype=F32)]
-        scratch += [buf(n, 16, 128)] * 2
+        scratch += [buf(n, 16, 128)]
     return pl.pallas_call(
         reduce_kernel,
         out_shape=[shape((128, 2048), BF16)]
-        + [shape((2, 4, 4, 4, n, 16, 128), BF16) for n in PARTS],
+        + [shape((2, 4, 4, 4, n, 16, 128), BF16) for n in SIZES],
         in_specs=[VMEM] + [HBM] * 3,
-        out_specs=[VMEM] + [HBM] * 3,
+        out_specs=[VMEM] + [HBM] * 6,
         scratch_shapes=scratch
         + [
-            pltpu.SemaphoreType.DMA((128,)),
-            pltpu.SemaphoreType.DMA((128,)),
-            pltpu.SemaphoreType.DMA((8,)),
+            pltpu.SemaphoreType.DMA((204,)),
+            pltpu.SemaphoreType.DMA((204,)),
+            pltpu.SemaphoreType.DMA((10,)),
         ],
         compiler_params=pltpu.CompilerParams(
             collective_id=1, has_side_effects=True, vmem_limit_bytes=60 * 2**20
@@ -655,61 +733,85 @@
     )(hidden, dqp, dkp, dvp)
 
 
-def widen_kernel(a, b, c, wk, wv):
-    for zi in range(4):
-        for core in range(2):
-            for tile in range(16):
-                row, column = tile // 4, tile % 4
-                if row == 0:
-                    value = a[core, zi, 0, 0, column]
-                elif row == 1:
-                    value = b[core, 0, 0, zi, column]
-                elif row == 2:
-                    value = c[core, 0, zi, 0, column]
-                elif column == 0:
-                    value = b[core, 0, 0, zi, 4]
-                elif column == 1:
-                    value = c[core, 0, zi, 0, 4]
-                else:
-                    value = a[core, zi, 0, 0, column + 2]
-                r0 = zi * 64 + row * 16
-                c0 = core * 256 + (column % 2) * 128
-                out = wk if column < 2 else wv
-                out[r0 : r0 + 16, c0 : c0 + 128] = value.astype(F32)
-
-
-def widen(a, b, c):
+def widen_kernel(*refs):
+    parts, (wk, wv), held, (wk_v, wv_v), (in_sems, out_sems) = (
+        refs[0:6], refs[6:8], refs[8:14], refs[14:16], refs[16:18]
+    )
+
+    def at(p, x, y, z):
+        places = {"x": x, "y": y, "z": z}
+        return tuple(places[axis] for axis in ORDERS[p % 3])
+
+    def loads(i):
+        x, y = lax.div(i, 4), lax.rem(i, 4)
+        spots = [(slice(None),) + at(p, x, y, slice(None)) for p in range(6)]
+        return [
+            pltpu.make_async_copy(parts[p].at[spot], held[p].at[spot], in_sems.at[p, i])
+            for p, spot in enumerate(spots)
+        ]
+
+    def stores(i):
+        rows = pl.ds(pl.multiple_of(i * 256, 256), 256)
+        return [
+            pltpu.make_async_copy(src.at[rows], dst.at[rows], out_sems.at[n, i])
+            for n, (src, dst) in enumerate(((wk_v, wk), (wv_v, wv)))
+        ]
+
+    def begin(i, _):
+        for copy in loads(i):
+            copy.start()
+        return 0
+
+    def block(i, _):
+        x, y = lax.div(i, 4), lax.rem(i, 4)
+        for copy in loads(i):
+            copy.wait()
+        for z in range(4):
+            r0 = pl.multiple_of(i * 256 + z * 64, 64)
+            for core in range(2):
+                for p in range(6):
+                    out = wk_v if p < 3 else wv_v
+                    for u, (row, column) in enumerate(PARTS[p // 3][p % 3]):
+                        value = held[p][(core,) + at(p, x, y, z) + (u,)]
+                        c0 = core * 256 + column * 128
+                        out[pl.ds(r0 + row * 16, 16), c0 : c0 + 128] = value.astype(F32)
+        for copy in stores(i):
+            copy.start()
+        return 0
+
+    def end(i, _):
+        for copy in stores(i):
+            copy.wait()
+        return 0
+
+    lax.fori_loop(0, 16, begin, 0)
+    lax.fori_loop(0, 16, block, 0)
+    lax.fori_loop(0, 16, end, 0)
+
+
+def widen(*parts):
     shape = jax.ShapeDtypeStruct
     return pl.pallas_call(
         widen_kernel,
-        grid=(16,),
         out_shape=[shape((4096, 512), F32)] * 2,
-        in_specs=[
-            pl.BlockSpec((2, 4, 1, 1, 6, 16, 128), lambda i: (0, 0, i // 4, i % 4, 0, 0, 0)),
-            pl.BlockSpec((2, 1, 1, 4, 5, 16, 128), lambda i: (0, i // 4, i % 4, 0, 0, 0, 0)),
-            pl.BlockSpec((2, 1, 4, 1, 5, 16, 128), lambda i: (0, i % 4, 0, i // 4, 0, 0, 0)),
+        in_specs=[HBM] * 6,
+        out_specs=[HBM] * 2,
+        scratch_shapes=[pltpu.VMEM((2, 4, 4, 4, n, 16, 128), BF16) for n in SIZES]
+        + [
+            pltpu.VMEM((4096, 512), F32),
+            pltpu.VMEM((4096, 512), F32),
+            pltpu.SemaphoreType.DMA((6, 16)),
+            pltpu.SemaphoreType.DMA((2, 16)),
         ],
-        out_specs=[pl.BlockSpec((256, 512), lambda i: (i, 0))] * 2,
         compiler_params=pltpu.CompilerParams(vmem_limit_bytes=60 * 2**20),
-    )(a, b, c)
+    )(*parts)
 
 
 def local(hidden, q, k, v, ao, do, lse, pos):
-    qg, dog, kg, vg, sg, pg = gather_all(q, do, k, v, ao, lse, pos[None, :])
-    kp = pg[:, :, :, 0, ::RUN].reshape(KEY_RUNS).astype(jnp.int32)
-    qp = sg[:, :, 16, ::RUN].reshape(QUERY_RUNS).astype(jnp.int32)
-    rank = jnp.sum(kp[None, :] < kp[:, None], axis=1, dtype=jnp.int32)
-    kplace = jnp.sum(
-        jnp.where(rank[None, :] == jnp.arange(KEY_RUNS)[:, None], kp[None, :], 0), axis=1, dtype=jnp.int32
-    )
-    qrank = jnp.sum(qp[None, :] < qp[:, None], axis=1, dtype=jnp.int32)
-    here = qrank[None, :] == jnp.arange(QUERY_RUNS)[:, None]
-    order = jnp.sum(jnp.where(here, jnp.arange(QUERY_RUNS)[None, :], 0), axis=1, dtype=jnp.int32)
-    qplace = jnp.sum(jnp.where(here, qp[None, :], 0), axis=1, dtype=jnp.int32)
-    reach = jnp.sum(kp[None, :] <= qplace[:, None], axis=1, dtype=jnp.int32)
-    dqp, dkp, dvp = attend(rank, order, reach, qplace, kplace, qg, dog, kg, vg, sg)
-    dq, a, b, c = reduce_all(hidden, dqp, dkp, dvp)
-    wk, wv = widen(a, b, c)
+    qg, dog, kg, vg, sg, pq, pk = gather_all(q, do, k, v, ao, lse.T, pos[None, :])
+    dqp, dkp, dvp = attend(pq, pk, qg, dog, kg, vg, sg)
+    dq, *parts = reduce_all(hidden, dqp, dkp, dvp)
+    wk, wv = widen(*parts)
     return dq, wk, wv
 
 

time: 242 us -> 225 us (0.930)
  local copies, waits for them, and re-layouts: 10.4 us -> 0.8 us
  Pallas kernels: 228 us -> 223 us
    slice x2 -> x0, local copies, waits for them, and re-layouts: 7.94 us -> none  [the longest x1 6.31 us: local(): kp = pg[:, :, :, 0, ::RUN].reshape(KEY_RUNS).astype(jnp.int32)]
    pallas_call x1, Pallas kernels: 55.9 us -> 49.1 us  [attend(): pl.pallas_call(attend_kernel, out_shape=[shape((4, 256, 1024), BF16), sha...]
    pallas_call x1, Pallas kernels: 114 us -> 120 us  [reduce_all(): pl.pallas_call(reduce_kernel, out_shape=[shape((128, 2048), BF16)] + [sha...]
    pallas_call x1, Pallas kernels: 13.6 us -> 9.38 us  [widen(): pl.pallas_call(widen_kernel, out_shape=[shape((4096, 512), F32)] * 2, in_...]
where the time goes in v2:
time: 225 us; the launch traced here: 224 us
  Pallas kernels  223 us (99%)
    pallas_call x1, Pallas kernels, reduce_all(): pl.pallas_call(reduce_kernel, out_shape=[shape((128, 2048), BF16)] + [sha...  120 us
    pallas_call x1, Pallas kernels, attend(): pl.pallas_call(attend_kernel, out_shape=[shape((4, 256, 1024), BF16), sha...  49.1 us
    pallas_call x1, Pallas kernels, gather_all(): pl.pallas_call(gather_kernel, out_shape=[shape((4, 256, 1024), BF16), sha...  44.7 us
    pallas_call x1, Pallas kernels, widen(): pl.pallas_call(widen_kernel, out_shape=[shape((4096, 512), F32)] * 2, in_...  9.38 us

profile of v2, /device:TPU:1, one launch (start us, length us, event | category | flops | bytes accessed | tf_op | source)
XLA Modules:
  0.0 224.2 jit_solution(16940075903338329197)
XLA Ops:
  0.6 44.7 %shard_map.103 = (bf16[4,256,1024]{2,1,0:T(8,128)(2,1)}, bf16[4,256,1024]{2,1,0:T(8,128)(2,1)}, bf16[4,4,256,256]{3,2,1,0:T(8,128)(2,1)}, bf16[4,4,256,256]{3,2,...) custom-call(bf16[128,2048]{1,0:T(8,128)(2,1)} %q.1, ...), custom_call_target="tpu_custom_call" | custom-call | tf_op jit(solution)/shard_map/pallas_call | solution.py:293
  45.3 49.1 %shard_map.104 = (bf16[4,256,1024]{2,1,0:T(8,128)(2,1)}, bf16[4,4,256,256]{3,2,1,0:T(8,128)(2,1)}, bf16[4,4,256,256]{3,2,1,0:T(8,128)(2,1)}) custom-call(s32[4,2,1,128]{3,2,1,0:T(1,128)} %get-tuple-element.22.pq, s32[4,4,2,1,128]{4,3,2,1,0:T(1,128)} %get-tuple-element.23.pk, bf16[4,256,1024]{2,1,0:T(8,128)(2,1)} %get-tuple-element.24.qg, ...), custom_call_target="tpu_custom_call" | custom-call | tf_op jit(solution)/shard_map/pallas_call | solution.py:514
  94.4 119.6 %shard_map.105 = (bf16[128,2048]{1,0:T(8,128)(2,1)}, bf16[2,4,4,4,3,16,128]{6,5,4,3,2,1,0:T(8,128)(2,1)}, bf16[2,4,4,4,3,16,128]{6,5,4,3,2,1,0:T(8,128)(2,1)}, b...) custom-call(bf16[128,4096]{1,0:T(8,128)(2,1)} %hidden.1, ...), custom_call_target="tpu_custom_call" | custom-call | tf_op jit(solution)/shard_map/pallas_call | solution.py:718
  214.0 0.0 copy-start
  214.0 9.4 %shard_map.106 = (f32[4096,512]{1,0:T(8,128)}, f32[4096,512]{1,0:T(8,128)}) custom-call(bf16[2,4,4,4,3,16,128]{6,5,4,3,2,1,0:T(8,128)(2,1)} %get-tuple-element.33.refs_0_, bf16[2,4,4,4,3,16,128]{6,5,4,3,2,1,0:T(8,128)(2,1)} %get-tuple-element.34.refs_1_, bf16[2,4,4,4,2,16,128]{6,5,4,3,2,1,0:T(8,128)(2,1)} %get-tuple-element.35.refs_2_, ...), custom_call_target="tpu_custom_call" | custom-call | tf_op jit(solution)/shard_map/pallas_call | solution.py:794
  223.4 0.0 copy-done
  223.4 0.8 copy.12
Async XLA Ops:
  214.0 9.4 %copy-start = (bf16[128,2048]{1,0:T(8,128)(2,1)S(1)}, bf16[128,2048]{1,0:T(8,128)(2,1)}, u32[]{:S(2)}) copy-start(bf16[128,2048]{1,0:T(8,128)(2,1)} %get-tuple-element.44) | copy-start | bytes 1572868

commit v3 on v2

--- a/solution.py
+++ b/solution.py
@@ -33,6 +33,7 @@
     (((0, 0), (0, 1), (3, 0)), ((1, 0), (1, 1), (3, 1)), ((2, 0), (2, 1))),
     (((0, 0), (0, 1), (3, 0)), ((1, 0), (1, 1)), ((2, 0), (2, 1), (3, 1))),
 )
+AXES = ((("y", "M"), ("M", "y")), (("M", "y"), ("M", "y")))
 SIZES = [len(tiles) for batch in PARTS for tiles in batch]
 
 
@@ -156,6 +157,12 @@
         ).astype(out.dtype)
 
 
+def late(rounds, chain):
+    for _ in range(rounds):
+        yield
+    yield from chain
+
+
 def together(*chains):
     chains = list(chains)
     while chains:
@@ -282,7 +289,7 @@
         keys_chain(k, kg, "M", "y"),
         keys_chain(v, vg, "y", "M"),
         queries_chain(q, qg),
-        queries_chain(do, dog),
+        late(2, queries_chain(do, dog)),
         stats_chain(),
     )
     net.finish()
@@ -306,8 +313,8 @@
         scratch_shapes=[
             pltpu.VMEM((128, 128), F32),
             pltpu.VMEM((2, 16, 128), F32),
-            pltpu.SemaphoreType.DMA((96,)),
-            pltpu.SemaphoreType.DMA((96,)),
+            pltpu.SemaphoreType.DMA((83,)),
+            pltpu.SemaphoreType.DMA((83,)),
             pltpu.SemaphoreType.DMA((8,)),
         ],
         compiler_params=pltpu.CompilerParams(
@@ -317,7 +324,7 @@
 
 
 def attend_kernel(
-    pq, pk, qg, dog, kg, vg, sg, dqp, dkp, dvp, order, reach, qplace, rank, kplace, found, found_s,
+    pq, pk, qg, dog, kg, vg, sg, dqp, dkp, dvp, order, reach, qplace, rank, origin, kplace, found, found_s,
     q_all, do_all, k_all, v_all, columns, dq_all, dk_all, dv_all,
     qs, dos, qt, dot_, lse_s, delta_s, dq_sum, dk_sum, dv_sum, in_sems, out_sems,
 ):
@@ -399,6 +406,7 @@
 
     def place_key(j, _):
         rank[j] = found_s[2, j]
+        origin[found_s[2, j]] = j
         kplace[found_s[2, j]] = key_place(j)
         return 0
 
@@ -414,6 +422,20 @@
     pltpu.make_async_copy(v_all, v_all, in_sems.at[1]).wait()
 
     per = CHUNK // RUN
+
+    def query_back(r):
+        i = order[r]
+        part = pl.ds(pl.multiple_of(lax.rem(i, 4) * RUN, RUN), RUN)
+        spot = pl.ds(pl.multiple_of(r * RUN, RUN), RUN)
+        return (pltpu.make_async_copy(dq_all.at[spot], dqp.at[lax.div(i, 4), part], out_sems.at[0]),)
+
+    def key_back(r):
+        j = origin[r]
+        spot = pl.ds(pl.multiple_of(r * RUN, RUN), RUN)
+        return (
+            pltpu.make_async_copy(dk_all.at[spot], at_run(dkp, j, True), out_sems.at[1]),
+            pltpu.make_async_copy(dv_all.at[spot], at_run(dvp, j, False), out_sems.at[2]),
+        )
 
     def unit(i, _):
         for u in range(UNIT):
@@ -434,21 +456,24 @@
             dot_[g] = dos[g].T
         dq_sum[...] = jnp.zeros_like(dq_sum)
         first, last = reach[i * UNIT], reach[i * UNIT + UNIT - 1]
-        whole, chunks = lax.div(first - 1, per), lax.div(last + per - 1, per)
-
-        def step(masked, chunk, _):
-            k0 = pl.multiple_of(chunk * CHUNK, CHUNK)
-            keys = pl.ds(k0, CHUNK)
+        whole = lax.div(first - 1, per)
+        rest = lax.rem(last, per)
+        chunks = lax.div(last, per) + jnp.where(rest > per // 2, 1, 0)
+        halves = jnp.where((rest > 0) & (rest <= per // 2), 1, 0)
+
+        def step(masked, size, base, chunk, _):
+            r0 = base + chunk * (size // RUN)
+            keys = pl.ds(pl.multiple_of(r0 * RUN, size), size)
             if masked:
                 row = lax.broadcasted_iota(jnp.int32, (rows, 1), 0)
                 qpos = lax.rem(row, RUN)
                 for u in range(UNIT):
                     inside = lax.div(row, SHARE * RUN) == u
                     qpos = qpos + jnp.where(inside, qplace[i * UNIT + u], 0)
-                column = lax.broadcasted_iota(jnp.int32, (1, CHUNK), 1)
+                column = lax.broadcasted_iota(jnp.int32, (1, size), 1)
                 kpos = lax.rem(column, RUN)
-                for u in range(per):
-                    kpos = kpos + jnp.where(lax.div(column, RUN) == u, kplace[chunk * per + u], 0)
+                for u in range(size // RUN):
+                    kpos = kpos + jnp.where(lax.div(column, RUN) == u, kplace[r0 + u], 0)
                 allowed = kpos <= qpos
             for g in range(GROUPS):
                 kk = k_all[keys, g * HEAD : (g + 1) * HEAD]
@@ -463,8 +488,9 @@
                 dk_sum[g, :, keys] += dot(qt[g], dscores, NN)
             return 0
 
-        lax.fori_loop(0, whole, functools.partial(step, False), 0)
-        lax.fori_loop(whole, chunks, functools.partial(step, True), 0)
+        lax.fori_loop(0, whole, functools.partial(step, False, CHUNK, 0), 0)
+        lax.fori_loop(whole, chunks, functools.partial(step, True, CHUNK, 0), 0)
+        lax.fori_loop(0, halves, functools.partial(step, True, CHUNK // 2, chunks * per), 0)
         for u in range(UNIT):
             r0 = pl.multiple_of((i * UNIT + u) * RUN, RUN)
             for g in range(GROUPS):
@@ -474,24 +500,11 @@
                     dq_all[pl.ds(r0, RUN), head * HEAD : (head + 1) * HEAD] = (
                         dq_sum[g, o : o + RUN, :] * SCALE
                     ).astype(BF16)
+            for copy in query_back(i * UNIT + u):
+                copy.start()
         return 0
 
     lax.fori_loop(0, QUERY_RUNS // UNIT, unit, 0)
-
-    def query_back(r):
-        i = order[r]
-        part = pl.ds(pl.multiple_of(lax.rem(i, 4) * RUN, RUN), RUN)
-        spot = pl.ds(pl.multiple_of(r * RUN, RUN), RUN)
-        return (pltpu.make_async_copy(dq_all.at[spot], dqp.at[lax.div(i, 4), part], out_sems.at[0]),)
-
-    def key_back(j):
-        spot = pl.ds(pl.multiple_of(rank[j] * RUN, RUN), RUN)
-        return (
-            pltpu.make_async_copy(dk_all.at[spot], at_run(dkp, j, True), out_sems.at[1]),
-            pltpu.make_async_copy(dv_all.at[spot], at_run(dvp, j, False), out_sems.at[2]),
-        )
-
-    lax.fori_loop(0, QUERY_RUNS, start(query_back), 0)
 
     def turn(chunk, _):
         keys = pl.ds(pl.multiple_of(chunk * CHUNK, CHUNK), CHUNK)
@@ -499,10 +512,12 @@
             columns_g = slice(g * HEAD, (g + 1) * HEAD)
             dk_all[keys, columns_g] = (dk_sum[g, :, keys] * SCALE).astype(BF16).T
             dv_all[keys, columns_g] = dv_sum[g, :, keys].astype(BF16).T
+        for u in range(per):
+            for copy in key_back(chunk * per + u):
+                copy.start()
         return 0
 
     lax.fori_loop(0, KEYS // CHUNK, turn, 0)
-    lax.fori_loop(0, KEY_RUNS, start(key_back), 0)
     pltpu.make_async_copy(dq_all, dq_all, out_sems.at[0]).wait()
     pltpu.make_async_copy(dk_all, dk_all, out_sems.at[1]).wait()
     pltpu.make_async_copy(dv_all, dv_all, out_sems.at[2]).wait()
@@ -524,6 +539,7 @@
             pltpu.SMEM((QUERY_RUNS,), jnp.int32),
             pltpu.SMEM((QUERY_RUNS,), jnp.int32),
             pltpu.SMEM((QUERY_RUNS,), jnp.int32),
+            pltpu.SMEM((KEY_RUNS,), jnp.int32),
             pltpu.SMEM((KEY_RUNS,), jnp.int32),
             pltpu.SMEM((KEY_RUNS,), jnp.int32),
             pltpu.VMEM((8, 128), jnp.int32),
@@ -584,8 +600,6 @@
             done.add(i)
 
     def queries_chain():
-        for _ in range(3):
-            yield
         first = net.scatter("L", dqp, dq_sums, lambda slot, part: (slot, part), 256, *dq_bufs, dq_own)
         next(first)
         yield
@@ -600,15 +614,14 @@
         copy.wait_recv()
 
     def terms_chain(batch, g):
-        for _ in range(batch):
-            yield
         hbm, sums = ((dkp, dk_sums), (dvp, dv_sums))[batch]
         relay, up, down, mid, inbox = term_bufs[batch * 2 + g]
-        axes = ("y", "M") if g == 0 else ("M", "y")
+        axes = AXES[batch][g]
         columns = pl.ds(g * HEAD, HEAD)
 
         def at(slot, part):
-            return (slot, part) + (slice(None), columns) if batch == g else (part, slot) + (slice(None), columns)
+            outer = axes[0] == ("y", "M")[batch]
+            return ((slot, part) if outer else (part, slot)) + (slice(None), columns)
 
         first = net.scatter(axes[0], hbm, sums, at, 4, relay, up, down, mid)
         next(first)
@@ -692,10 +705,10 @@
 
     chains = []
     for batch in range(2):
-        chains += [terms_chain(batch, 0), terms_chain(batch, 1)]
+        chains += [terms_chain(batch, g) for g in range(GROUPS)]
         chains += [hidden_chain()] if batch == 0 else []
         chains += [project_chain(batch)] + [part_chain(batch, p) for p in range(3)]
-    together(*chains, queries_chain())
+    together(*chains, late(1, queries_chain()))
     net.finish()
 
 
@@ -723,8 +736,8 @@
         out_specs=[VMEM] + [HBM] * 6,
         scratch_shapes=scratch
         + [
-            pltpu.SemaphoreType.DMA((204,)),
-            pltpu.SemaphoreType.DMA((204,)),
+            pltpu.SemaphoreType.DMA((200,)),
+            pltpu.SemaphoreType.DMA((200,)),
             pltpu.SemaphoreType.DMA((10,)),
         ],
         compiler_params=pltpu.CompilerParams(

time: 225 us -> 211 us (0.938)
  Pallas kernels: 223 us -> 209 us
    pallas_call x1, Pallas kernels: 120 us -> 98.1 us  [reduce_all(): pl.pallas_call(reduce_kernel, out_shape=[shape((128, 2048), BF16)] + [sha...]
    pallas_call x1, Pallas kernels: 49.1 us -> 62.6 us  [attend(): pl.pallas_call(attend_kernel, out_shape=[shape((4, 256, 1024), BF16), sha...]
    pallas_call x1, Pallas kernels: 44.7 us -> 39.3 us  [gather_all(): pl.pallas_call(gather_kernel, out_shape=[shape((4, 256, 1024), BF16), sha...]
where the time goes in v3:
time: 211 us
  Pallas kernels  209 us (99%)
    pallas_call x1, Pallas kernels, reduce_all(): pl.pallas_call(reduce_kernel, out_shape=[shape((128, 2048), BF16)] + [sha...  98.1 us
    pallas_call x1, Pallas kernels, attend(): pl.pallas_call(attend_kernel, out_shape=[shape((4, 256, 1024), BF16), sha...  62.6 us
    pallas_call x1, Pallas kernels, gather_all(): pl.pallas_call(gather_kernel, out_shape=[shape((4, 256, 1024), BF16), sha...  39.3 us
    pallas_call x1, Pallas kernels, widen(): pl.pallas_call(widen_kernel, out_shape=[shape((4096, 512), F32)] * 2, in_...  9.38 us

profile of v3, /device:TPU:1, one launch (start us, length us, event | category | flops | bytes accessed | tf_op | source)
XLA Modules:
  0.0 210.9 jit_solution(15184972468031966323)
XLA Ops:
  0.6 39.3 %shard_map.103 = (bf16[4,256,1024]{2,1,0:T(8,128)(2,1)}, bf16[4,256,1024]{2,1,0:T(8,128)(2,1)}, bf16[4,4,256,256]{3,2,1,0:T(8,128)(2,1)}, bf16[4,4,256,256]{3,2,...) custom-call(bf16[128,2048]{1,0:T(8,128)(2,1)} %q.1, ...), custom_call_target="tpu_custom_call" | custom-call | tf_op jit(solution)/shard_map/pallas_call | solution.py:300
  39.9 62.6 %shard_map.104 = (bf16[4,256,1024]{2,1,0:T(8,128)(2,1)}, bf16[4,4,256,256]{3,2,1,0:T(8,128)(2,1)}, bf16[4,4,256,256]{3,2,1,0:T(8,128)(2,1)}) custom-call(s32[4,2,1,128]{3,2,1,0:T(1,128)} %get-tuple-element.22.pq, s32[4,4,2,1,128]{4,3,2,1,0:T(1,128)} %get-tuple-element.23.pk, bf16[4,256,1024]{2,1,0:T(8,128)(2,1)} %get-tuple-element.24.qg, ...), custom_call_target="tpu_custom_call" | custom-call | tf_op jit(solution)/shard_map/pallas_call | solution.py:529
  102.6 98.1 %shard_map.105 = (bf16[128,2048]{1,0:T(8,128)(2,1)}, bf16[2,4,4,4,3,16,128]{6,5,4,3,2,1,0:T(8,128)(2,1)}, bf16[2,4,4,4,3,16,128]{6,5,4,3,2,1,0:T(8,128)(2,1)}, b...) custom-call(bf16[128,4096]{1,0:T(8,128)(2,1)} %hidden.1, ...), custom_call_target="tpu_custom_call" | custom-call | tf_op jit(solution)/shard_map/pallas_call | solution.py:731
  200.7 0.0 copy-start
  200.7 9.4 %shard_map.106 = (f32[4096,512]{1,0:T(8,128)}, f32[4096,512]{1,0:T(8,128)}) custom-call(bf16[2,4,4,4,3,16,128]{6,5,4,3,2,1,0:T(8,128)(2,1)} %get-tuple-element.33.refs_0_, bf16[2,4,4,4,3,16,128]{6,5,4,3,2,1,0:T(8,128)(2,1)} %get-tuple-element.34.refs_1_, bf16[2,4,4,4,2,16,128]{6,5,4,3,2,1,0:T(8,128)(2,1)} %get-tuple-element.35.refs_2_, ...), custom_call_target="tpu_custom_call" | custom-call | tf_op jit(solution)/shard_map/pallas_call | solution.py:807
  210.1 0.0 copy-done
  210.1 0.8 copy.12
Async XLA Ops:
  200.7 9.4 %copy-start = (bf16[128,2048]{1,0:T(8,128)(2,1)S(1)}, bf16[128,2048]{1,0:T(8,128)(2,1)}, u32[]{:S(2)}) copy-start(bf16[128,2048]{1,0:T(8,128)(2,1)} %get-tuple-element.44) | copy-start | bytes 1572868

commit v4 on v3

--- a/solution.py
+++ b/solution.py
@@ -174,12 +174,17 @@
 
 
 def gather_kernel(
-    q, do, k, v, do_v, ao, lse, pos, qg, dog, kg, vg, sg, pq, pk, stats, mine, send_sems, recv_sems, own_sems
+    q, do, k, v, ao, lse, pos, qg, dog, kg, vg, sg, pq, pk, do_v, ao_v, stats, mine, send_sems, recv_sems, own_sems
 ):
     place = Place()
     net = Net(place, send_sems, recv_sems)
     y, c, l, m = place.at["y"], place.c, place.at["L"], place.at["M"]
     twin = place.device(other=True)
+    loads = [
+        pltpu.make_async_copy(src, dst, own_sems.at[7 + n]) for n, (src, dst) in enumerate(((do, do_v), (ao, ao_v)))
+    ]
+    for copy in loads:
+        copy.start()
     net.greet()
     first, second = (pl.multiple_of(i * 128, 128) for i in (c, 1 - c))
 
@@ -259,9 +264,11 @@
     def stats_chain():
         kept = [keep(pos, pk.at[y, m, c]), keep(pos, pq.at[l, c])]
         from_twin = [net.send(pos, pk.at[y, l, c], twin), net.send(pos, pq.at[m, c], twin)]
+        for copy in loads:
+            copy.wait()
         for h in range(16):
             columns = slice(h * HEAD, (h + 1) * HEAD)
-            product = do_v[:, columns].astype(F32) * ao[:, columns].astype(F32)
+            product = do_v[:, columns].astype(F32) * ao_v[:, columns].astype(F32)
             stats[:, h : h + 1] = jnp.sum(product, axis=1, keepdims=True)
         turned = stats[...].T
         for i in range(2):
@@ -308,19 +315,21 @@
             shape((4, 2, 1, 128), jnp.int32),
             shape((4, 4, 2, 1, 128), jnp.int32),
         ],
-        in_specs=[HBM] * 4 + [VMEM] * 4,
+        in_specs=[HBM] * 5 + [VMEM] * 2,
         out_specs=[HBM] * 7,
         scratch_shapes=[
+            pltpu.VMEM((128, 2048), BF16),
+            pltpu.VMEM((128, 2048), BF16),
             pltpu.VMEM((128, 128), F32),
             pltpu.VMEM((2, 16, 128), F32),
             pltpu.SemaphoreType.DMA((83,)),
             pltpu.SemaphoreType.DMA((83,)),
-            pltpu.SemaphoreType.DMA((8,)),
+            pltpu.SemaphoreType.DMA((9,)),
         ],
         compiler_params=pltpu.CompilerParams(
             collective_id=0, has_side_effects=True, vmem_limit_bytes=60 * 2**20
         ),
-    )(q, do, k, v, do, ao, lse, pos)
+    )(q, do, k, v, ao, lse, pos)
 
 
 def attend_kernel(
@@ -576,17 +585,18 @@
         return taken
 
     wg = take(6)
-    h_twin, ht, dkv, dq_sums, dk_sums, dv_sums = take(6)
+    h_own, h_twin, ht, dkv, dq_sums, dk_sums, dv_sums = take(7)
     dq_bufs, dq_own = take(3), take(1)[0]
     term_bufs = [take(5) for _ in range(4)]
-    part_bufs = [take(9) for _ in range(6)]
+    part_bufs = [take(8) for _ in range(6)]
+    held = take(6)
     send_sems, recv_sems, own_sems = rest
     place = Place()
     net = Net(place, send_sems, recv_sems)
     c = place.c
     twin = place.device(other=True)
     loads = []
-    for src, dst in ((dkp, dk_sums), (dvp, dv_sums), (dqp, dq_sums)):
+    for src, dst in ((dkp, dk_sums), (dvp, dv_sums), (dqp, dq_sums), (hidden, h_own)):
         loads.append(pltpu.make_async_copy(src, dst, own_sems.at[len(loads)]))
         loads[-1].start()
     net.greet()
@@ -607,7 +617,7 @@
         yield from first
         columns = pl.ds(pl.multiple_of(c * 1024, 1024), 1024)
         copy = net.send(dq_own.at[theirs], dq.at[:, columns], twin)
-        own = pltpu.make_async_copy(dq_own.at[rows], dq.at[:, columns], own_sems.at[3])
+        own = pltpu.make_async_copy(dq_own.at[rows], dq.at[:, columns], own_sems.at[16])
         own.start()
         yield
         own.wait()
@@ -635,9 +645,10 @@
     def hidden_chain():
         copy = net.send(hidden, h_twin, twin)
         yield
+        loaded(3)
         copy.wait_recv()
-        ht[:, 0:128] = jnp.where(c == 0, hidden[...], h_twin[...]).T
-        ht[:, 128:256] = jnp.where(c == 0, h_twin[...], hidden[...]).T
+        ht[:, 0:128] = jnp.where(c == 0, h_own[...], h_twin[...]).T
+        ht[:, 128:256] = jnp.where(c == 0, h_twin[...], h_own[...]).T
         done.add("hidden")
 
     def project_chain(batch):
@@ -663,18 +674,16 @@
     def part_chain(batch, p):
         while ("project", batch) not in done:
             yield
-        order, whole = ORDERS[p], wg[batch * 3 + p]
-        terms, relay, up, down, mid, inbox, mid2, inbox2, total = part_bufs[batch * 3 + p]
+        n = batch * 3 + p
+        order, whole, out = ORDERS[p], held[n], wg[n]
+        terms, relay, up, down, mid, inbox, mid2, inbox2 = part_bufs[n]
         at = [place.at[axis] for axis in order]
+        mine = whole.at[c]
         yield from net.scatter(
             order[0], terms, terms, lambda slot, part: (slot, part), 4, relay, up, down, mid
         )
         yield from net.scatter_direct(order[1], mid, inbox, mid2)
-        yield from net.scatter_direct(order[2], mid2, inbox2, total)
-        mine = whole.at[c]
-        own = pltpu.make_async_copy(total, mine.at[at[0], at[1], at[2]], own_sems.at[4 + batch * 3 + p])
-        own.start()
-        own.wait()
+        yield from net.scatter_direct(order[2], mid2, inbox2, mine.at[at[0], at[1], at[2]])
         copies = net.cast(order[2], mine.at[at[0], at[1], at[2]])
         yield
         for copy in copies:
@@ -687,8 +696,12 @@
         def ref(slot, part):
             return mine.at[slot, part]
 
+        def keep(core, which, slot):
+            pltpu.make_async_copy(whole.at[core, slot], out.at[core, slot], own_sems.at[4 + 2 * n + which]).start()
+
         def share(slot):
-            return net.send(mine.at[slot], mine.at[slot], twin)
+            keep(c, 0, slot)
+            return slot, net.send(mine.at[slot], mine.at[slot], twin)
 
         pair = net.pair(order[0], mine.at[at[0]], mine.at[at[0]])
         shares = [share(at[0])]
@@ -700,8 +713,12 @@
             copy.wait_recv()
         shares.append(share(wrap(at[0] + 2)))
         yield
-        for copy in shares:
-            copy.wait_recv()
+        for slot, copy in shares:
+            copy.wait_recv()
+            keep(1 - c, 1, slot)
+        yield
+        for which, core in enumerate((c, 1 - c)):
+            pltpu.make_async_copy(whole.at[core], out.at[core], own_sems.at[4 + 2 * n + which]).wait()
 
     chains = []
     for batch in range(2):
@@ -718,7 +735,7 @@
     def buf(*dims, dtype=BF16):
         return pltpu.VMEM(dims, dtype)
 
-    scratch = [buf(128, 4096), buf(4096, 256), buf(256, 512)]
+    scratch = [buf(128, 4096), buf(128, 4096), buf(4096, 256), buf(256, 512)]
     scratch += [buf(4, 256, 1024), buf(4, 4, 256, 256), buf(4, 4, 256, 256)]
     scratch += [buf(256, 1024)] * 4
     for _ in range(4):
@@ -727,18 +744,18 @@
         scratch += [buf(4, 4, 4, n, 16, 128)]
         scratch += [buf(4, 4, n, 16, 128)] * 4 + [buf(3, 4, n, 16, 128)]
         scratch += [buf(4, n, 16, 128, dtype=F32), buf(3, n, 16, 128, dtype=F32)]
-        scratch += [buf(n, 16, 128)]
+    scratch += [buf(2, 4, 4, 4, n, 16, 128) for n in SIZES]
     return pl.pallas_call(
         reduce_kernel,
         out_shape=[shape((128, 2048), BF16)]
         + [shape((2, 4, 4, 4, n, 16, 128), BF16) for n in SIZES],
-        in_specs=[VMEM] + [HBM] * 3,
-        out_specs=[VMEM] + [HBM] * 6,
+        in_specs=[HBM] * 4,
+        out_specs=[HBM] * 7,
         scratch_shapes=scratch
         + [
             pltpu.SemaphoreType.DMA((200,)),
             pltpu.SemaphoreType.DMA((200,)),
-            pltpu.SemaphoreType.DMA((10,)),
+            pltpu.SemaphoreType.DMA((17,)),
         ],
         compiler_params=pltpu.CompilerParams(
             collective_id=1, has_side_effects=True, vmem_limit_bytes=60 * 2**20

time: 211 us -> 210 us (level)
    pallas_call x1, Pallas kernels: 62.6 us -> 54 us  [attend(): pl.pallas_call(attend_kernel, out_shape=[shape((4, 256, 1024), BF16), sha...]
    pallas_call x1, Pallas kernels: 98.1 us -> 106 us  [reduce_all(): pl.pallas_call(reduce_kernel, out_shape=[shape((128, 2048), BF16)] + [sha...]
where the time goes in v4:
time: 210 us
  Pallas kernels  208 us (99%)
    pallas_call x1, Pallas kernels, reduce_all(): pl.pallas_call(reduce_kernel, out_shape=[shape((128, 2048), BF16)] + [sha...  106 us
    pallas_call x1, Pallas kernels, attend(): pl.pallas_call(attend_kernel, out_shape=[shape((4, 256, 1024), BF16), sha...  54 us
    pallas_call x1, Pallas kernels, gather_all(): pl.pallas_call(gather_kernel, out_shape=[shape((4, 256, 1024), BF16), sha...  38.8 us
    pallas_call x1, Pallas kernels, widen(): pl.pallas_call(widen_kernel, out_shape=[shape((4096, 512), F32)] * 2, in_...  9.38 us

profile of v4, /device:TPU:1, one launch (start us, length us, event | category | flops | bytes accessed | tf_op | source)
XLA Modules:
  0.0 209.6 jit_solution(13006926517042560660)
XLA Ops:
  0.6 38.8 %shard_map.103 = (bf16[4,256,1024]{2,1,0:T(8,128)(2,1)}, bf16[4,256,1024]{2,1,0:T(8,128)(2,1)}, bf16[4,4,256,256]{3,2,1,0:T(8,128)(2,1)}, bf16[4,4,256,256]{3,2,...) custom-call(bf16[128,2048]{1,0:T(8,128)(2,1)} %q.1, ...), custom_call_target="tpu_custom_call" | custom-call | tf_op jit(solution)/shard_map/pallas_call | solution.py:307
  39.4 54.0 %shard_map.104 = (bf16[4,256,1024]{2,1,0:T(8,128)(2,1)}, bf16[4,4,256,256]{3,2,1,0:T(8,128)(2,1)}, bf16[4,4,256,256]{3,2,1,0:T(8,128)(2,1)}) custom-call(s32[4,2,1,128]{3,2,1,0:T(1,128)} %get-tuple-element.22.pq, s32[4,4,2,1,128]{4,3,2,1,0:T(1,128)} %get-tuple-element.23.pk, bf16[4,256,1024]{2,1,0:T(8,128)(2,1)} %get-tuple-element.24.qg, ...), custom_call_target="tpu_custom_call" | custom-call | tf_op jit(solution)/shard_map/pallas_call | solution.py:538
  93.4 106.0 %shard_map.105 = (bf16[128,2048]{1,0:T(8,128)(2,1)}, bf16[2,4,4,4,3,16,128]{6,5,4,3,2,1,0:T(8,128)(2,1)}, bf16[2,4,4,4,3,16,128]{6,5,4,3,2,1,0:T(8,128)(2,1)}, b...) custom-call(bf16[128,4096]{1,0:T(8,128)(2,1)} %hidden.1, ...), custom_call_target="tpu_custom_call" | custom-call | tf_op jit(solution)/shard_map/pallas_call | solution.py:748
  199.4 0.0 copy-start
  199.4 9.4 %shard_map.106 = (f32[4096,512]{1,0:T(8,128)}, f32[4096,512]{1,0:T(8,128)}) custom-call(bf16[2,4,4,4,3,16,128]{6,5,4,3,2,1,0:T(8,128)(2,1)} %get-tuple-element.33.refs_0_, bf16[2,4,4,4,3,16,128]{6,5,4,3,2,1,0:T(8,128)(2,1)} %get-tuple-element.34.refs_1_, bf16[2,4,4,4,2,16,128]{6,5,4,3,2,1,0:T(8,128)(2,1)} %get-tuple-element.35.refs_2_, ...), custom_call_target="tpu_custom_call" | custom-call | tf_op jit(solution)/shard_map/pallas_call | solution.py:824
  208.8 0.0 copy-done
  208.8 0.8 copy.12
Async XLA Ops:
  199.4 9.4 %copy-start = (bf16[128,2048]{1,0:T(8,128)(2,1)S(1)}, bf16[128,2048]{1,0:T(8,128)(2,1)}, u32[]{:S(2)}) copy-start(bf16[128,2048]{1,0:T(8,128)(2,1)} %get-tuple-element.44) | copy-start | bytes 1572868

commit v5 on v4

--- a/solution.py
+++ b/solution.py
@@ -28,10 +28,10 @@
 VMEM = pl.BlockSpec(memory_space=pltpu.VMEM)
 SMEM = pl.BlockSpec(memory_space=pltpu.SMEM)
 HBM = pl.BlockSpec(memory_space=pltpu.HBM)
-ORDERS = ("zxy", "xyz", "yzx")
+ORDERS = ("zyx", "xzy", "yxz")
 PARTS = (
-    (((0, 0), (0, 1), (3, 0)), ((1, 0), (1, 1), (3, 1)), ((2, 0), (2, 1))),
     (((0, 0), (0, 1), (3, 0)), ((1, 0), (1, 1)), ((2, 0), (2, 1), (3, 1))),
+    (((0, 0), (0, 1)), ((1, 0), (1, 1), (3, 0)), ((2, 0), (2, 1), (3, 1))),
 )
 AXES = ((("y", "M"), ("M", "y")), (("M", "y"), ("M", "y")))
 SIZES = [len(tiles) for batch in PARTS for tiles in batch]

time: 210 us -> 211 us (level)
    pallas_call x1, Pallas kernels: 54 us -> 57.6 us  [attend(): pl.pallas_call(attend_kernel, out_shape=[shape((4, 256, 1024), BF16), sha...]
    pallas_call x1, Pallas kernels: 106 us -> 104 us  [reduce_all(): pl.pallas_call(reduce_kernel, out_shape=[shape((128, 2048), BF16)] + [sha...]
where the time goes in v5:
time: 211 us
  Pallas kernels  210 us (100%)
    pallas_call x1, Pallas kernels, reduce_all(): pl.pallas_call(reduce_kernel, out_shape=[shape((128, 2048), BF16)] + [sha...  104 us
    pallas_call x1, Pallas kernels, attend(): pl.pallas_call(attend_kernel, out_shape=[shape((4, 256, 1024), BF16), sha...  57.6 us
    pallas_call x1, Pallas kernels, gather_all(): pl.pallas_call(gather_kernel, out_shape=[shape((4, 256, 1024), BF16), sha...  38.8 us
    pallas_call x1, Pallas kernels, widen(): pl.pallas_call(widen_kernel, out_shape=[shape((4096, 512), F32)] * 2, in_...  9.37 us

profile of v5, /device:TPU:1, one launch (start us, length us, event | category | flops | bytes accessed | tf_op | source)
XLA Modules:
  0.0 211.1 jit_solution(18410347638096696998)
XLA Ops:
  0.6 38.8 %shard_map.103 = (bf16[4,256,1024]{2,1,0:T(8,128)(2,1)}, bf16[4,256,1024]{2,1,0:T(8,128)(2,1)}, bf16[4,4,256,256]{3,2,1,0:T(8,128)(2,1)}, bf16[4,4,256,256]{3,2,...) custom-call(bf16[128,2048]{1,0:T(8,128)(2,1)} %q.1, ...), custom_call_target="tpu_custom_call" | custom-call | tf_op jit(solution)/shard_map/pallas_call | solution.py:307
  39.4 57.6 %shard_map.104 = (bf16[4,256,1024]{2,1,0:T(8,128)(2,1)}, bf16[4,4,256,256]{3,2,1,0:T(8,128)(2,1)}, bf16[4,4,256,256]{3,2,1,0:T(8,128)(2,1)}) custom-call(s32[4,2,1,128]{3,2,1,0:T(1,128)} %get-tuple-element.22.pq, s32[4,4,2,1,128]{4,3,2,1,0:T(1,128)} %get-tuple-element.23.pk, bf16[4,256,1024]{2,1,0:T(8,128)(2,1)} %get-tuple-element.24.qg, ...), custom_call_target="tpu_custom_call" | custom-call | tf_op jit(solution)/shard_map/pallas_call | solution.py:538
  97.1 103.8 %shard_map.105 = (bf16[128,2048]{1,0:T(8,128)(2,1)}, bf16[2,4,4,4,3,16,128]{6,5,4,3,2,1,0:T(8,128)(2,1)}, bf16[2,4,4,4,2,16,128]{6,5,4,3,2,1,0:T(8,128)(2,1)}, b...) custom-call(bf16[128,4096]{1,0:T(8,128)(2,1)} %hidden.1, ...), custom_call_target="tpu_custom_call" | custom-call | tf_op jit(solution)/shard_map/pallas_call | solution.py:748
  200.9 0.0 copy-start
  200.9 9.4 %shard_map.106 = (f32[4096,512]{1,0:T(8,128)}, f32[4096,512]{1,0:T(8,128)}) custom-call(bf16[2,4,4,4,3,16,128]{6,5,4,3,2,1,0:T(8,128)(2,1)} %get-tuple-element.33.refs_0_, bf16[2,4,4,4,2,16,128]{6,5,4,3,2,1,0:T(8,128)(2,1)} %get-tuple-element.34.refs_1_, bf16[2,4,4,4,3,16,128]{6,5,4,3,2,1,0:T(8,128)(2,1)} %get-tuple-element.35.refs_2_, ...), custom_call_target="tpu_custom_call" | custom-call | tf_op jit(solution)/shard_map/pallas_call | solution.py:824
  210.3 0.0 copy-done
  210.3 0.8 copy.12
Async XLA Ops:
  200.9 9.4 %copy-start = (bf16[128,2048]{1,0:T(8,128)(2,1)S(1)}, bf16[128,2048]{1,0:T(8,128)(2,1)}, u32[]{:S(2)}) copy-start(bf16[128,2048]{1,0:T(8,128)(2,1)} %get-tuple-element.44) | copy-start | bytes 1572868

commit v6 on v5

--- a/solution.py
+++ b/solution.py
@@ -468,7 +468,8 @@
         whole = lax.div(first - 1, per)
         rest = lax.rem(last, per)
         chunks = lax.div(last, per) + jnp.where(rest > per // 2, 1, 0)
-        halves = jnp.where((rest > 0) & (rest <= per // 2), 1, 0)
+        halves = jnp.where((rest > per // 4) & (rest <= per // 2), 1, 0)
+        quarters = jnp.where((rest > 0) & (rest <= per // 4), 1, 0)
 
         def step(masked, size, base, chunk, _):
             r0 = base + chunk * (size // RUN)
@@ -500,6 +501,7 @@
         lax.fori_loop(0, whole, functools.partial(step, False, CHUNK, 0), 0)
         lax.fori_loop(whole, chunks, functools.partial(step, True, CHUNK, 0), 0)
         lax.fori_loop(0, halves, functools.partial(step, True, CHUNK // 2, chunks * per), 0)
+        lax.fori_loop(0, quarters, functools.partial(step, True, CHUNK // 4, chunks * per), 0)
         for u in range(UNIT):
             r0 = pl.multiple_of((i * UNIT + u) * RUN, RUN)
             for g in range(GROUPS):

time: 211 us -> 210 us (level)
    pallas_call x1, Pallas kernels: 57.6 us -> 47.2 us  [attend(): pl.pallas_call(attend_kernel, out_shape=[shape((4, 256, 1024), BF16), sha...]
    pallas_call x1, Pallas kernels: 104 us -> 114 us  [reduce_all(): pl.pallas_call(reduce_kernel, out_shape=[shape((128, 2048), BF16)] + [sha...]
where the time goes in v6:
time: 210 us
  Pallas kernels  209 us (100%)
    pallas_call x1, Pallas kernels, reduce_all(): pl.pallas_call(reduce_kernel, out_shape=[shape((128, 2048), BF16)] + [sha...  114 us
    pallas_call x1, Pallas kernels, attend(): pl.pallas_call(attend_kernel, out_shape=[shape((4, 256, 1024), BF16), sha...  47.2 us
    pallas_call x1, Pallas kernels, gather_all(): pl.pallas_call(gather_kernel, out_shape=[shape((4, 256, 1024), BF16), sha...  38.8 us
    pallas_call x1, Pallas kernels, widen(): pl.pallas_call(widen_kernel, out_shape=[shape((4096, 512), F32)] * 2, in_...  9.37 us

profile of v6, /device:TPU:1, one launch (start us, length us, event | category | flops | bytes accessed | tf_op | source)
XLA Modules:
  0.0 210.4 jit_solution(4653191663379480820)
XLA Ops:
  0.6 38.8 %shard_map.103 = (bf16[4,256,1024]{2,1,0:T(8,128)(2,1)}, bf16[4,256,1024]{2,1,0:T(8,128)(2,1)}, bf16[4,4,256,256]{3,2,1,0:T(8,128)(2,1)}, bf16[4,4,256,256]{3,2,...) custom-call(bf16[128,2048]{1,0:T(8,128)(2,1)} %q.1, ...), custom_call_target="tpu_custom_call" | custom-call | tf_op jit(solution)/shard_map/pallas_call | solution.py:307
  39.4 47.2 %shard_map.104 = (bf16[4,256,1024]{2,1,0:T(8,128)(2,1)}, bf16[4,4,256,256]{3,2,1,0:T(8,128)(2,1)}, bf16[4,4,256,256]{3,2,1,0:T(8,128)(2,1)}) custom-call(s32[4,2,1,128]{3,2,1,0:T(1,128)} %get-tuple-element.22.pq, s32[4,4,2,1,128]{4,3,2,1,0:T(1,128)} %get-tuple-element.23.pk, bf16[4,256,1024]{2,1,0:T(8,128)(2,1)} %get-tuple-element.24.qg, ...), custom_call_target="tpu_custom_call" | custom-call | tf_op jit(solution)/shard_map/pallas_call | solution.py:540
  86.6 113.6 %shard_map.105 = (bf16[128,2048]{1,0:T(8,128)(2,1)}, bf16[2,4,4,4,3,16,128]{6,5,4,3,2,1,0:T(8,128)(2,1)}, bf16[2,4,4,4,2,16,128]{6,5,4,3,2,1,0:T(8,128)(2,1)}, b...) custom-call(bf16[128,4096]{1,0:T(8,128)(2,1)} %hidden.1, ...), custom_call_target="tpu_custom_call" | custom-call | tf_op jit(solution)/shard_map/pallas_call | solution.py:750
  200.2 0.0 copy-start
  200.2 9.4 %shard_map.106 = (f32[4096,512]{1,0:T(8,128)}, f32[4096,512]{1,0:T(8,128)}) custom-call(bf16[2,4,4,4,3,16,128]{6,5,4,3,2,1,0:T(8,128)(2,1)} %get-tuple-element.33.refs_0_, bf16[2,4,4,4,2,16,128]{6,5,4,3,2,1,0:T(8,128)(2,1)} %get-tuple-element.34.refs_1_, bf16[2,4,4,4,3,16,128]{6,5,4,3,2,1,0:T(8,128)(2,1)} %get-tuple-element.35.refs_2_, ...), custom_call_target="tpu_custom_call" | custom-call | tf_op jit(solution)/shard_map/pallas_call | solution.py:826
  209.6 0.0 copy-done
  209.6 0.8 copy.12
Async XLA Ops:
  200.2 9.4 %copy-start = (bf16[128,2048]{1,0:T(8,128)(2,1)S(1)}, bf16[128,2048]{1,0:T(8,128)(2,1)}, u32[]{:S(2)}) copy-start(bf16[128,2048]{1,0:T(8,128)(2,1)} %get-tuple-element.44) | copy-start | bytes 1572868
